TPU v7x, 256 devices: a whole 4x4x8 slice. The times are simulated.
256 devices in a mesh: segment: 8 (over x, core), expert: 32 (over y, z).
Axes of the slice: x: 4, y: 4, z: 8, core: 2. Of those that a mesh axis runs over, the one named last changes fastest.
Arguments:
- tokens: bfloat16 [8, 4096, 7168], P('segment', 'expert'), may hold values from -6 to 6
- entering: bfloat16 [4096, 7168], P('expert'), may hold values from -6 to 6
- norm_gain: float32 [8, 7168], P('segment'), may hold values from 0.1 to 1.9
- gate_up: bfloat16 [8, 32, 896, 8, 2, 128], P('segment', 'expert'), may hold values from -0.0625 to 0.0625
- down_proj: bfloat16 [8, 32, 1024, 896], P('segment', 'expert'), may hold values from -0.1875 to 0.1875
- expert_ids: int32 [8, 4096, 1], P('segment', 'expert'), may hold values from 0 to 3; in each aligned block of 128 rows (0 to 127, 128 to 255, ..., all dimensions but the last counted through in order) at most 36 rows name the same one
- gate_weights: float32 [8, 4096, 1], P('segment', 'expert'), may hold values from 0.5 to 2
Outputs:
- segment_outputs: bfloat16 [2, 8, 4096, 7168], P(None, 'segment', 'expert')
Inputs may be any that keep to these rules, and one draw needn't show every extreme that they name: `expert_ids`: among the 128 tokens that one device holds in one segment, at most 36 name the same expert, and in some of these blocks one expert is named by exactly 36.
All inputs are finite; a program needn't handle non-finite values.
Results may differ from a plain program's by a relative error of at most 0.008.
Values may be sent and summed in bfloat16 or wider, within the bound.
No kernel may reach another device: no remote copies, remote signals or barrier semaphores. Data moves between devices by JAX's collectives and lax.ppermute only.
A program may use at most 128 MiB of HBM per device.

v0:
```python
import jax
import jax.numpy as jnp
from jax import lax
from jax.sharding import PartitionSpec as P

SPLIT = 8


EPSILON = 1e-06


def swapped(value, axis, apart):
    mask = 2**apart
    pairs = [(source, source ^ mask) for source in range(lax.axis_size(axis))]
    return lax.ppermute(value, axis, pairs)


def passed_along(shard, axis, by):
    count = lax.axis_size(axis)
    pairs = [(i, i + by) for i in range(count) if 0 <= i + by < count]
    return lax.ppermute(shard, axis, pairs)


def rms_normed(stream, gain_row):
    values = stream.astype(jnp.float32)
    mean_sq = jnp.mean(values * values, axis=-1, keepdims=True)
    return (values * lax.rsqrt(mean_sq + EPSILON) * gain_row).astype(jnp.bfloat16)


def per_device(tokens, entering, norm_gain, gate_up, down_proj, expert_ids, gate_weights):
    lane_count = lax.axis_size("expert")
    groups = lane_count // SPLIT
    segment_index = lax.axis_index("segment")
    lane_bits = lax.axis_index("expert") % SPLIT
    tok_rows, model_width = entering.shape
    top_count = expert_ids.shape[2]
    slot_cap = min(tok_rows, 9 * tok_rows * top_count // (8 * groups))
    piece_width = model_width // SPLIT
    block_width = down_proj.shape[2] // SPLIT
    levels = SPLIT.bit_length() - 1
    flat_ids = expert_ids[0].reshape(tok_rows * top_count)
    member = (flat_ids[:, None] == jnp.arange(groups, dtype=jnp.int32)[None, :]).astype(jnp.int32)
    slot_of = jnp.sum((jnp.cumsum(member, axis=0) - 1) * member, axis=1)
    target = flat_ids * slot_cap + slot_of
    chosen = (jnp.arange(groups * slot_cap, dtype=jnp.int32)[:, None] == target[None, :]).astype(
        jnp.float32
    )
    chosen = chosen.reshape(groups, slot_cap, tok_rows, top_count)
    pick_table = jnp.sum(chosen, axis=3).astype(jnp.bfloat16)
    token_weight = jnp.sum(gate_weights[0], axis=1)
    bit_order = tuple(range(levels - 1, -1, -1))
    kept_block = jnp.zeros((), jnp.int32)
    for bit_pos in bit_order:
        kept_block = kept_block * 2 + (lane_bits >> bit_pos & 1)

    def moe_layer(stream):
        normed = rms_normed(stream, norm_gain[0])
        outgoing = jnp.einsum(
            "gcr,rjp->gjcp",
            pick_table,
            normed.reshape(tok_rows, SPLIT, piece_width),
            preferred_element_type=jnp.float32,
        )
        outgoing = outgoing.astype(jnp.bfloat16).reshape(lane_count, slot_cap, piece_width)
        arrived = lax.all_to_all(outgoing, "expert", split_axis=0, concat_axis=0, tiled=True)
        slot_rows = arrived.reshape(lane_count * slot_cap, piece_width)
        weights_in = gate_up[0, 0].reshape(piece_width, 2 * SPLIT * block_width)
        partial_value = jnp.dot(slot_rows, weights_in, preferred_element_type=jnp.float32)
        for bit_pos in bit_order:
            half_cols = partial_value.shape[1] // 2
            upper_bit = lane_bits >> bit_pos & 1
            keep_part = lax.dynamic_slice_in_dim(partial_value, upper_bit * half_cols, half_cols, 1)
            give_part = lax.dynamic_slice_in_dim(
                partial_value, (1 - upper_bit) * half_cols, half_cols, 1
            )
            partial_value = keep_part + swapped(give_part, "expert", bit_pos)
        hidden = (
            jax.nn.silu(partial_value[:, :block_width]) * partial_value[:, block_width:]
        ).astype(jnp.bfloat16)
        down_full = down_proj[0, 0]
        for bit_pos in reversed(bit_order):
            partner_part = swapped(hidden, "expert", bit_pos)
            upper_set = lane_bits >> bit_pos & 1 == 1
            hidden = jnp.where(
                upper_set,
                jnp.concatenate([partner_part, hidden], axis=1),
                jnp.concatenate([hidden, partner_part], axis=1),
            )
        expert_out = jnp.dot(hidden, down_full, preferred_element_type=jnp.float32)
        expert_out = expert_out.astype(jnp.bfloat16).reshape(lane_count, slot_cap, piece_width)
        returned = lax.all_to_all(expert_out, "expert", split_axis=0, concat_axis=0, tiled=True)
        returned = returned.reshape(groups, SPLIT, slot_cap, piece_width)
        selected = jnp.einsum(
            "gcr,gjcp->rjp", pick_table, returned, preferred_element_type=jnp.float32
        )
        weighted = selected * token_weight[:, None, None]
        return (stream.astype(jnp.float32) + weighted.reshape(tok_rows, model_width)).astype(
            jnp.bfloat16
        )

    first_result = moe_layer(tokens[0])
    passed = passed_along(first_result, "segment", 1)
    second_input = jnp.where(segment_index == 0, entering, passed)
    second_result = moe_layer(second_input)
    return jnp.stack([first_result, second_result])[:, None]


def solution(mesh):
    in_specs = (
        P("segment", "expert", None),
        P("expert", None),
        P("segment", None),
        P("segment", "expert", None, None, None, None),
        P("segment", "expert", None, None),
        P("segment", "expert", None),
        P("segment", "expert", None),
    )
    out_specs = P(None, "segment", "expert", None)
    return jax.shard_map(
        per_device, mesh=mesh, in_specs=in_specs, out_specs=out_specs, check_vma=False
    )
```

profile of v0, /device:TPU:2, one launch (start us, length us, event | category | flops | bytes accessed | tf_op | source)
XLA Modules:
  0.0 1265.3 jit_solution(8480592947466638130)
XLA Ops:
  2.6 3.9 copy.26
  8.9 3.9 copy.27
  14.1 2.9 convert_bitcast_fusion.1
  19.7 11.6 all-to-all-start
  31.3 7.1 reshape_squeeze.8
  38.5 46.9 %all-to-all-done = bf16[32,36,896]{2,1,0:T(8,128)(2,1)} async-done(((bf16[32,36,896]{2,1,0:T(8,128)(2,1)}), bf16[32,36,896]{2,1,0:T(8,128)(2,1)}, u32[]{:S(2)}, u32[]{:S(2)}) %all-to-all-start) | async-done | bytes 2064416 | tf_op jit(solution)/shard_map/all_to_all | solution.py:65
  85.4 3.9 reshape.114
  89.3 7.7 fusion.44
  97.0 3.2 constant_dynamic-slice_fusion.4
  103.2 207.8 %collective-permute-done = f32[1152,1024]{1,0:T(8,128)} collective-permute-done((f32[1152,1024]{1,0:T(8,128)}, f32[1152,1024]{1,0:T(8,128)}, u32[]{:S(2)}, u32[]{:S(2)}) %collective-permute-start) | collective-permute-done | bytes 4718624 | tf_op jit(solution)/shard_map/ppermute | solution.py:15
  311.0 4.8 dynamic-slice_add_fusion.1
  318.8 102.3 %collective-permute-done.1 = f32[1152,512]{1,0:T(8,128)} collective-permute-done((f32[1152,512]{1,0:T(8,128)}, f32[1152,512]{1,0:T(8,128)}, u32[]{:S(2)}, u32[]{:S(2)}) %collective-permute-start.1) | collective-permute-done | bytes 2359328 | tf_op jit(solution)/shard_map/ppermute | solution.py:15
  421.2 2.9 dynamic-slice_add_fusion.3
  426.0 25.6 %collective-permute-done.2 = f32[1152,256]{1,0:T(8,128)} collective-permute-done((f32[1152,256]{1,0:T(8,128)S(1)}, f32[1152,256]{1,0:T(8,128)}, u32[]{:S(2)}, u32[]{:S(2)}) %collective-permute-start.2) | collective-permute-done | bytes 1179680 | tf_op jit(solution)/shard_map/ppermute | solution.py:15
  454.4 6.0 collective-permute-done.3
  460.6 4.2 collective-permute-start.4
  464.7 24.7 %collective-permute-done.4 = bf16[1152,256]{1,0:T(8,128)(2,1)S(1)} collective-permute-done((bf16[1152,256]{1,0:T(8,128)(2,1)S(1)}, bf16[1152,256]{1,0:T(8,128)(2,1)S(1)}, u32[]{:S(2)}, u32[]{:S(2)}) %collective-permute-start.4) | collective-permute-done | bytes 589856 | tf_op jit(solution)/shard_map/ppermute | solution.py:15
  490.7 5.8 collective-permute-start.5
  496.5 51.7 %collective-permute-done.5 = bf16[1152,512]{1,0:T(8,128)(2,1)S(1)} collective-permute-done((bf16[1152,512]{1,0:T(8,128)(2,1)}, bf16[1152,512]{1,0:T(8,128)(2,1)S(1)}, u32[]{:S(2)}, u32[]{:S(2)}) %collective-permute-start.5) | collective-permute-done | bytes 1179680 | tf_op jit(solution)/shard_map/ppermute | solution.py:15
  548.2 5.6 convolution_convert_fusion.1
  553.8 3.9 reshape.115
  557.8 62.3 %all_to_all.20 = bf16[32,36,896]{2,1,0:T(8,128)(2,1)S(1)} all-to-all(bf16[32,36,896]{2,1,0:T(8,128)(2,1)} %reshape.115), channel_id=1, replica_groups=mesh['segment'=8,'expert'=32] {'expert'}, dimensions={0} | all-to-all | bytes 4128768 | tf_op jit(solution)/shard_map/all_to_all | solution.py:91
  620.0 2.6 bitcast_multiply_fusion.1
  622.6 5.0 copy.32
  627.6 4.2 fusion.4
  633.7 3.9 copy.34
  637.6 19.0 %collective-permute-done.6 = bf16[128,7168]{0,1:T(8,128)(2,1)} collective-permute-done((bf16[128,7168]{0,1:T(8,128)(2,1)}, bf16[128,7168]{0,1:T(8,128)(2,1)}, u32[]{:S(2)}, u32[]{:S(2)}) %collective-permute-start.6) | collective-permute-done | bytes 1835040 | tf_op jit(solution)/shard_map/ppermute | solution.py:21
  659.1 3.0 fusion.2
  664.8 69.9 %all_to_all.21 = bf16[32,36,896]{2,1,0:T(8,128)(2,1)} all-to-all(bf16[32,36,896]{2,1,0:T(8,128)(2,1)S(1)} %copy.37), channel_id=1, replica_groups=mesh['segment'=8,'expert'=32] {'expert'}, dimensions={0} | all-to-all | bytes 4128768 | tf_op jit(solution)/shard_map/all_to_all | solution.py:65
  734.7 4.0 reshape.121
  738.7 7.7 fusion.45
  748.3 203.1 %collective-permute-done.7 = f32[1152,1024]{1,0:T(8,128)S(1)} collective-permute-done((f32[1152,1024]{1,0:T(8,128)S(1)}, f32[1152,1024]{1,0:T(8,128)S(1)}, u32[]{:S(2)}, u32[]{:S(2)}) %collective-permute-start.7) | collective-permute-done | bytes 4718624 | tf_op jit(solution)/shard_map/ppermute | solution.py:15
  953.2 3.1 collective-permute-start.8
  956.3 101.1 %collective-permute-done.8 = f32[1152,512]{1,0:T(8,128)S(1)} collective-permute-done((f32[1152,512]{1,0:T(8,128)S(1)}, f32[1152,512]{1,0:T(8,128)S(1)}, u32[]{:S(2)}, u32[]{:S(2)}) %collective-permute-start.8) | collective-permute-done | bytes 2359328 | tf_op jit(solution)/shard_map/ppermute | solution.py:15
  1058.2 27.0 %collective-permute-done.9 = f32[1152,256]{1,0:T(8,128)S(1)} collective-permute-done((f32[1152,256]{1,0:T(8,128)S(1)}, f32[1152,256]{1,0:T(8,128)S(1)}, u32[]{:S(2)}, u32[]{:S(2)}) %collective-permute-start.9) | collective-permute-done | bytes 1179680 | tf_op jit(solution)/shard_map/ppermute | solution.py:15
  1085.9 6.9 collective-permute-done.10
  1093.1 26.0 %collective-permute-done.11 = bf16[1152,256]{1,0:T(8,128)(2,1)S(1)} collective-permute-done((bf16[1152,256]{1,0:T(8,128)(2,1)S(1)}, bf16[1152,256]{1,0:T(8,128)(2,1)S(1)}, u32[]{:S(2)}, u32[]{:S(2)}) %collective-permute-start.11) | collective-permute-done | bytes 589856 | tf_op jit(solution)/shard_map/ppermute | solution.py:15
  1119.5 2.5 collective-permute-start.12
  1122.0 53.5 %collective-permute-done.12 = bf16[1152,512]{1,0:T(8,128)(2,1)S(1)} collective-permute-done((bf16[1152,512]{1,0:T(8,128)(2,1)S(1)}, bf16[1152,512]{1,0:T(8,128)(2,1)S(1)}, u32[]{:S(2)}, u32[]{:S(2)}) %collective-permute-start.12) | collective-permute-done | bytes 1179680 | tf_op jit(solution)/shard_map/ppermute | solution.py:15
  1175.5 3.8 convolution_convert_fusion
  1179.3 3.9 reshape.122
  1183.2 7.6 all-to-all-start.3
  1190.8 4.2 fusion.5
  1195.0 49.7 %all-to-all-done.3 = bf16[32,36,896]{2,1,0:T(8,128)(2,1)} async-done(((bf16[32,36,896]{2,1,0:T(8,128)(2,1)}), bf16[32,36,896]{2,1,0:T(8,128)(2,1)}, u32[]{:S(2)}, u32[]{:S(2)}) %all-to-all-start.3) | async-done | bytes 2064416 | tf_op jit(solution)/shard_map/all_to_all | solution.py:91
  1244.7 4.2 bitcast_multiply_fusion
  1249.0 5.0 copy.40
  1254.0 3.1 fusion.3
  1259.2 5.9 copy.41
  (58 shorter events, 36.1 us)
Async XLA Ops:
  0.0 548.2 %copy-start = (bf16[1,1,1024,896]{3,2,1,0:T(8,128)(2,1)S(1)}, bf16[1,1,1024,896]{3,2,1,0:T(8,128)(2,1)}, u32[]{:S(2)}) copy-start(bf16[1,1,1024,896]{3,2,1,0:T(8,128)(2,1)} %param.11) | copy-start | bytes 5505028
  8.9 4.5 copy-start.6
  19.7 65.7 %all-to-all-start = ((bf16[32,36,896]{2,1,0:T(8,128)(2,1)}), bf16[32,36,896]{2,1,0:T(8,128)(2,1)}, u32[]{:S(2)}, u32[]{:S(2)}) async-start(bf16[32,36,896]{2,1,0:T(8,128)(2,1)} %copy.29), calls=%async_computation | async-start | bytes 4587520 | tf_op jit(solution)/shard_map/all_to_all | solution.py:65
  97.0 5.0 copy-start.4
  102.0 209.0 %collective-permute-start = (f32[1152,1024]{1,0:T(8,128)}, f32[1152,1024]{1,0:T(8,128)}, u32[]{:S(2)}, u32[]{:S(2)}) collective-permute-start(f32[1152,1024]{1,0:T(8,128)} %constant_dynamic-slice_fusion.4), channel_id=1, source_target_pairs={{0,4},{1,5},{2,6},{3,7},{4,0},{5,1},{6,2},{7,3},{8,12},{9,13},{10,... | collective-permute-start | bytes 14155784 | tf_op jit(solution)/shard_map/ppermute | solution.py:15
  315.9 3.0 copy-start.1
  318.8 102.3 %collective-permute-start.1 = (f32[1152,512]{1,0:T(8,128)}, f32[1152,512]{1,0:T(8,128)}, u32[]{:S(2)}, u32[]{:S(2)}) collective-permute-start(f32[1152,512]{1,0:T(8,128)} %constant_dynamic-slice_fusion.3), channel_id=1, source_target_pairs={{0,2},{1,3},{2,0},{3,1},{4,6},{5,7},{6,4},{7,5},{8,10},{9,11},{10,... | collective-permute-start | bytes 7077896 | tf_op jit(solution)/shard_map/ppermute | solution.py:15
  424.1 1.4 copy-start.3
  425.6 25.9 %collective-permute-start.2 = (f32[1152,256]{1,0:T(8,128)S(1)}, f32[1152,256]{1,0:T(8,128)}, u32[]{:S(2)}, u32[]{:S(2)}) collective-permute-start(f32[1152,256]{1,0:T(8,128)S(1)} %constant_dynamic-slice_fusion.2), channel_id=1, source_target_pairs={{0,1},{1,0},{2,3},{3,2},{4,5},{5,4},{6,7},{7,6},{8,9},{9,8},{10,11... | collective-permute-start | bytes 3538952 | tf_op jit(solution)/shard_map/ppermute | solution.py:15
  453.5 6.8 collective-permute-start.3
  460.6 28.9 %collective-permute-start.4 = (bf16[1152,256]{1,0:T(8,128)(2,1)S(1)}, bf16[1152,256]{1,0:T(8,128)(2,1)S(1)}, u32[]{:S(2)}, u32[]{:S(2)}) collective-permute-start(bf16[1152,256]{1,0:T(8,128)(2,1)S(1)} %maximum_select_fusion.6), channel_id=1, source_target_pairs={{0,2},{1,3},{2,0},{3,1},{4,6},{5,7},{6,4},{7,5},{8,10},{9,11},{10,... | collective-permute-start | bytes 1769480 | tf_op jit(solution)/shard_map/ppermute | solution.py:15
  490.7 57.5 %collective-permute-start.5 = (bf16[1152,512]{1,0:T(8,128)(2,1)}, bf16[1152,512]{1,0:T(8,128)(2,1)S(1)}, u32[]{:S(2)}, u32[]{:S(2)}) collective-permute-start(bf16[1152,512]{1,0:T(8,128)(2,1)} %maximum_select_fusion.4), channel_id=1, source_target_pairs={{0,4},{1,5},{2,6},{3,7},{4,0},{5,1},{6,2},{7,3},{8,12},{9,13},{10,... | collective-permute-start | bytes 3538952 | tf_op jit(solution)/shard_map/ppermute | solution.py:15
  557.8 62.3 %copy-start.7 = (f32[1,128,1]{1,2,0:T(1,128)S(1)}, f32[1,128,1]{1,2,0:T(1,128)}, u32[]{:S(2)}) copy-start(f32[1,128,1]{1,2,0:T(1,128)} %param.13) | copy-start | bytes 1540
  631.8 24.8 %collective-permute-start.6 = (bf16[128,7168]{0,1:T(8,128)(2,1)}, bf16[128,7168]{0,1:T(8,128)(2,1)}, u32[]{:S(2)}, u32[]{:S(2)}) collective-permute-start(bf16[128,7168]{0,1:T(8,128)(2,1)} %fusion.4), channel_id=1, source_target_pairs={{0,32},{32,64},{64,96},{96,128},{128,160},{160,192},{192,224},{1,3... | collective-permute-start | bytes 5505032 | tf_op jit(solution)/shard_map/ppermute | solution.py:21
  659.1 4.3 copy-start.2
  746.8 204.6 %collective-permute-start.7 = (f32[1152,1024]{1,0:T(8,128)S(1)}, f32[1152,1024]{1,0:T(8,128)S(1)}, u32[]{:S(2)}, u32[]{:S(2)}) collective-permute-start(f32[1152,1024]{1,0:T(8,128)S(1)} %constant_dynamic-slice_fusion.1), channel_id=1, source_target_pairs={{0,4},{1,5},{2,6},{3,7},{4,0},{5,1},{6,2},{7,3},{8,12},{9,13},{10,... | collective-permute-start | bytes 14155784 | tf_op jit(solution)/shard_map/ppermute | solution.py:15
  953.2 104.2 %collective-permute-start.8 = (f32[1152,512]{1,0:T(8,128)S(1)}, f32[1152,512]{1,0:T(8,128)S(1)}, u32[]{:S(2)}, u32[]{:S(2)}) collective-permute-start(f32[1152,512]{1,0:T(8,128)S(1)} %constant_dynamic-slice_fusion), channel_id=1, source_target_pairs={{0,2},{1,3},{2,0},{3,1},{4,6},{5,7},{6,4},{7,5},{8,10},{9,11},{10,... | collective-permute-start | bytes 7077896 | tf_op jit(solution)/shard_map/ppermute | solution.py:15
  1058.1 27.1 %collective-permute-start.9 = (f32[1152,256]{1,0:T(8,128)S(1)}, f32[1152,256]{1,0:T(8,128)S(1)}, u32[]{:S(2)}, u32[]{:S(2)}) collective-permute-start(f32[1152,256]{1,0:T(8,128)S(1)} %constant_dynamic-slice_fusion.5), channel_id=1, source_target_pairs={{0,1},{1,0},{2,3},{3,2},{4,5},{5,4},{6,7},{7,6},{8,9},{9,8},{10,11... | collective-permute-start | bytes 3538952 | tf_op jit(solution)/shard_map/ppermute | solution.py:15
  1085.6 7.2 collective-permute-start.10
  1093.0 26.1 %collective-permute-start.11 = (bf16[1152,256]{1,0:T(8,128)(2,1)S(1)}, bf16[1152,256]{1,0:T(8,128)(2,1)S(1)}, u32[]{:S(2)}, u32[]{:S(2)}) collective-permute-start(bf16[1152,256]{1,0:T(8,128)(2,1)S(1)} %maximum_select_fusion.7), channel_id=1, source_target_pairs={{0,2},{1,3},{2,0},{3,1},{4,6},{5,7},{6,4},{7,5},{8,10},{9,11},{10,... | collective-permute-start | bytes 1769480 | tf_op jit(solution)/shard_map/ppermute | solution.py:15
  1119.5 56.0 %collective-permute-start.12 = (bf16[1152,512]{1,0:T(8,128)(2,1)S(1)}, bf16[1152,512]{1,0:T(8,128)(2,1)S(1)}, u32[]{:S(2)}, u32[]{:S(2)}) collective-permute-start(bf16[1152,512]{1,0:T(8,128)(2,1)S(1)} %maximum_select_fusion.5), channel_id=1, source_target_pairs={{0,4},{1,5},{2,6},{3,7},{4,0},{5,1},{6,2},{7,3},{8,12},{9,13},{10,... | collective-permute-start | bytes 3538952 | tf_op jit(solution)/shard_map/ppermute | solution.py:15
  1183.2 61.5 %all-to-all-start.3 = ((bf16[32,36,896]{2,1,0:T(8,128)(2,1)}), bf16[32,36,896]{2,1,0:T(8,128)(2,1)}, u32[]{:S(2)}, u32[]{:S(2)}) async-start(bf16[32,36,896]{2,1,0:T(8,128)(2,1)} %reshape.122), calls=%async_computation.3 | async-start | bytes 4587520 | tf_op jit(solution)/shard_map/all_to_all | solution.py:91
  1254.0 3.1 copy-start.5
where the time goes:
time: 1270 us
  waiting for transfers between devices  951 us (75%)
  blocking collectives  132 us (10%)
  local copies, waits for them, and re-layouts  65.4 us (5%)
  starting transfers between devices  41.1 us (3%)
  other arithmetic  39 us (3%)
  matrix products  35.9 us (3%)
    ppermute x12, waiting for transfers between devices, swapped(): return lax.ppermute(value, axis, pairs)  836 us
    all_to_all x1, blocking collectives, moe_layer(): lax.all_to_all(outgoing, 'expert', split_axis=0, concat_axis=0, tiled=True)  69.9 us
    all_to_all x1, blocking collectives, moe_layer(): lax.all_to_all(expert_out, 'expert', split_axis=0, concat_axis=0, tiled=T...  62.3 us
    all_to_all x1, waiting for transfers between devices, moe_layer(): lax.all_to_all(expert_out, 'expert', split_axis=0, concat_axis=0, tiled=T...  49.7 us
    all_to_all x1, waiting for transfers between devices, moe_layer(): lax.all_to_all(outgoing, 'expert', split_axis=0, concat_axis=0, tiled=True)  46.9 us
  transfers between devices with their start and end apart: 15, of which 15 were waited for; matrix products, arithmetic and copies ran while one was open for 1% of the time, Pallas kernels for 0%

commit v1 on v0

v1 whole, which is shorter than its diff:
```python
import jax
import jax.numpy as jnp
from jax import lax
from jax.sharding import Mesh, PartitionSpec as P

EPSILON = 1e-06


def shifted(value, axis, by):
    count = lax.axis_size(axis)
    return lax.ppermute(value, axis, [(i, (i + by) % count) for i in range(count)])


def passed_along(shard, axis, by):
    count = lax.axis_size(axis)
    pairs = [(i, i + by) for i in range(count) if 0 <= i + by < count]
    return lax.ppermute(shard, axis, pairs)


def rms_normed(stream, gain_row):
    values = stream.astype(jnp.float32)
    mean_sq = jnp.mean(values * values, axis=-1, keepdims=True)
    return (values * lax.rsqrt(mean_sq + EPSILON) * gain_row).astype(jnp.bfloat16)


def per_device(tokens, entering, norm_gain, gate_up, down_proj, expert_ids, gate_weights):
    split = lax.axis_size("z")
    groups = lax.axis_size("y")
    segment_index = lax.axis_index("segment")
    place = lax.axis_index("z")
    tok_rows, model_width = entering.shape
    slot_cap = 9 * tok_rows // (8 * groups)
    piece_width = model_width // split
    hidden_width = down_proj.shape[2]
    flat_ids = expert_ids[0].reshape(tok_rows)
    member = (flat_ids[:, None] == jnp.arange(groups, dtype=jnp.int32)[None, :]).astype(jnp.int32)
    slot_of = jnp.sum((jnp.cumsum(member, axis=0) - 1) * member, axis=1)
    target = flat_ids * slot_cap + slot_of
    pick_table = (
        (jnp.arange(groups * slot_cap, dtype=jnp.int32)[:, None] == target[None, :])
        .astype(jnp.bfloat16)
        .reshape(groups, slot_cap, tok_rows)
    )
    token_weight = gate_weights[0][:, 0]
    weights_in = gate_up[0, 0].reshape(piece_width, 2 * hidden_width)
    weights_out = down_proj[0, 0]
    half = hidden_width
    far = split // 2

    def moe_layer(stream):
        normed = rms_normed(stream, norm_gain[0])
        outgoing = jnp.einsum(
            "gcr,rjp->jgcp",
            pick_table,
            normed.reshape(tok_rows, split, piece_width),
            preferred_element_type=jnp.float32,
        )
        outgoing = outgoing.astype(jnp.bfloat16).reshape(split * groups, slot_cap, piece_width)
        arrived = lax.all_to_all(outgoing, ("z", "y"), split_axis=0, concat_axis=0, tiled=True)
        arrived = arrived.reshape(split, groups * slot_cap, piece_width)

        def partial_sums(offset):
            rows = lax.dynamic_index_in_dim(arrived, (place + offset) % split, 0, False)
            return jnp.dot(rows, weights_in, preferred_element_type=jnp.float32)

        opposite = partial_sums(far).astype(jnp.bfloat16)
        low_up, high_down = opposite[:, :half], opposite[:, half:]
        high_up = low_down = None
        for step in range(far - 1, 0, -1):
            low_up = shifted(low_up, "z", 1)
            high_down = shifted(high_down, "z", -1)
            if high_up is not None:
                high_up = shifted(high_up, "z", 1)
                low_down = shifted(low_down, "z", -1)
            ahead, behind = partial_sums(step), partial_sums(-step)
            low_up = (low_up.astype(jnp.float32) + ahead[:, :half]).astype(jnp.bfloat16)
            high_down = (high_down.astype(jnp.float32) + behind[:, half:]).astype(jnp.bfloat16)
            if high_up is None:
                high_up = ahead[:, half:].astype(jnp.bfloat16)
                low_down = behind[:, :half].astype(jnp.bfloat16)
            else:
                high_up = (high_up.astype(jnp.float32) + ahead[:, half:]).astype(jnp.bfloat16)
                low_down = (low_down.astype(jnp.float32) + behind[:, :half]).astype(jnp.bfloat16)
        low_up, high_up = shifted(low_up, "z", 1), shifted(high_up, "z", 1)
        low_down, high_down = shifted(low_down, "z", -1), shifted(high_down, "z", -1)
        own = partial_sums(0)
        low = own[:, :half] + low_up.astype(jnp.float32) + low_down.astype(jnp.float32)
        high = own[:, half:] + high_up.astype(jnp.float32) + high_down.astype(jnp.float32)

        def activated(sums):
            pairs = sums.reshape(groups * slot_cap, -1, 2, 128)
            return (jax.nn.silu(pairs[:, :, 0]) * pairs[:, :, 1]).astype(jnp.bfloat16).reshape(
                groups * slot_cap, half // 2
            )

        hidden = jnp.concatenate([activated(low), activated(high)], axis=1)
        results = jnp.zeros((split, groups * slot_cap, piece_width), jnp.bfloat16)

        def projected(results, rows, offset):
            block = jnp.dot(rows, weights_out, preferred_element_type=jnp.float32)
            return lax.dynamic_update_index_in_dim(
                results, block.astype(jnp.bfloat16), (place + offset) % split, 0
            )

        from_below = from_above = hidden
        results = projected(results, hidden, 0)
        for step in range(1, far):
            from_below = shifted(from_below, "z", 1)
            from_above = shifted(from_above, "z", -1)
            results = projected(results, from_below, -step)
            results = projected(results, from_above, step)
        left = shifted(from_below[:, : half // 2], "z", 1)
        right = shifted(from_above[:, half // 2 :], "z", -1)
        results = projected(results, jnp.concatenate([left, right], axis=1), far)
        returned = lax.all_to_all(
            results.reshape(split * groups, slot_cap, piece_width),
            ("z", "y"),
            split_axis=0,
            concat_axis=0,
            tiled=True,
        )
        returned = returned.reshape(split, groups, slot_cap, piece_width)
        selected = jnp.einsum(
            "gcr,jgcp->rjp", pick_table, returned, preferred_element_type=jnp.float32
        )
        weighted = selected * token_weight[:, None, None]
        return (stream.astype(jnp.float32) + weighted.reshape(tok_rows, model_width)).astype(
            jnp.bfloat16
        )

    first_result = moe_layer(tokens[0])
    passed = passed_along(first_result, "segment", 1)
    second_input = jnp.where(segment_index == 0, entering, passed)
    second_result = moe_layer(second_input)
    return jnp.stack([first_result, second_result])[:, None]


def solution(mesh):
    segments, experts = mesh.devices.shape
    split = 8
    fine = Mesh(mesh.devices.reshape(segments, experts // split, split), ("segment", "y", "z"))
    both = ("y", "z")
    in_specs = (
        P("segment", both, None),
        P(both, None),
        P("segment", None),
        P("segment", both, None, None, None, None),
        P("segment", both, None, None),
        P("segment", both, None),
        P("segment", both, None),
    )
    out_specs = P(None, "segment", both, None)
    return jax.shard_map(
        per_device, mesh=fine, in_specs=in_specs, out_specs=out_specs, check_vma=False
    )
```

time: 1270 us -> 544 us (0.43)
  waiting for transfers between devices: 951 us -> 177 us
  starting transfers between devices: 41.1 us -> 86.2 us
  matrix products: 35.9 us -> 50.7 us
    ppermute x12 -> x44, waiting for transfers between devices: 836 us -> 69.8 us  [shifted(): lax.ppermute(value, axis, [(i, (i + by) % count) for i in range(count)])]
    ppermute x12 -> x44, starting transfers between devices: 20 us -> 66.5 us  [shifted(): lax.ppermute(value, axis, [(i, (i + by) % count) for i in range(count)])]
    dot_general x8 -> x36, matrix products: 35.9 us -> 50.7 us  [the longest x16 19.6 us: partial_sums(): return jnp.dot(rows, weights_in, preferred_element_type=jnp.float32)]
  transfers between devices with their start and end apart: 15 -> 47, of which waited for: 15 -> 28; matrix products, arithmetic and copies ran while one was open for 1% -> 9% of each run, Pallas kernels for 0% -> 0%
where the time goes in v1:
time: 544 us; the launch traced here: 534 us
  waiting for transfers between devices  177 us (33%)
  blocking collectives  122 us (22%)
  starting transfers between devices  86.2 us (16%)
  local copies, waits for them, and re-layouts  68.2 us (13%)
  matrix products  50.7 us (9%)
  other arithmetic  28.3 us (5%)
    ppermute x44, waiting for transfers between devices, shifted(): lax.ppermute(value, axis, [(i, (i + by) % count) for i in range(count)])  69.8 us
    ppermute x44, starting transfers between devices, shifted(): lax.ppermute(value, axis, [(i, (i + by) % count) for i in range(count)])  66.5 us
    all_to_all x1, blocking collectives, moe_layer(): lax.all_to_all(results.reshape(split * groups, slot_cap, piece_width), ('...  61.3 us
    all_to_all x1, blocking collectives, moe_layer(): lax.all_to_all(outgoing, ('z', 'y'), split_axis=0, concat_axis=0, tiled=T...  60.2 us
    all_to_all x1, waiting for transfers between devices, moe_layer(): lax.all_to_all(outgoing, ('z', 'y'), split_axis=0, concat_axis=0, tiled=T...  47 us
    all_to_all x1, waiting for transfers between devices, moe_layer(): lax.all_to_all(results.reshape(split * groups, slot_cap, piece_width), ('...  41.5 us
    dot_general x16, matrix products, partial_sums(): return jnp.dot(rows, weights_in, preferred_element_type=jnp.float32)  19.6 us
    dot_general x16, matrix products, projected(): block = jnp.dot(rows, weights_out, preferred_element_type=jnp.float32)  19.2 us
  transfers between devices with their start and end apart: 47, of which 28 were waited for; matrix products, arithmetic and copies ran while one was open for 9% of the time, Pallas kernels for 0%

profile of v1, /device:TPU:2, one launch (start us, length us, event | category | flops | bytes accessed | tf_op | source)
XLA Modules:
  0.0 533.5 jit_solution(12524424416953222959)
XLA Ops:
  2.6 3.9 copy.10
  8.9 3.9 copy.11
  14.0 4.3 convolution_convert_fusion.3
  18.3 11.6 %all-to-all-start = ((bf16[32,36,896]{2,1,0:T(8,128)(2,1)}), bf16[32,36,896]{2,1,0:T(8,128)(2,1)}, u32[]{:S(2)}, u32[]{:S(2)}) async-start(bf16[32,36,896]{2,1,0:T(8,128)(2,1)} %bitcast.407), calls=%async_computation | async-start | bytes 4587520 | tf_op jit(solution)/shard_map/all_to_all | solution.py:59
  30.0 7.1 %reshape_squeeze.7 = bf16[896,2048]{1,0:T(8,128)(2,1)} reshape(bf16[1,1,896,8,2,128]{5,4,3,2,1,0:T(2,128)(2,1)} %param.10) | data formatting | bytes 7340032 | tf_op jit(solution)/shard_map/reshape;squeeze | solution.py:45
  37.1 47.0 %all-to-all-done = bf16[32,36,896]{2,1,0:T(8,128)(2,1)} async-done(((bf16[32,36,896]{2,1,0:T(8,128)(2,1)}), bf16[32,36,896]{2,1,0:T(8,128)(2,1)}, u32[]{:S(2)}, u32[]{:S(2)}) %all-to-all-start) | async-done | bytes 2064416 | tf_op jit(solution)/shard_map/all_to_all | solution.py:59
  84.2 4.0 reshape.132
  102.7 5.5 %collective-permute-done.10 = bf16[144,1024]{1,0:T(8,128)(2,1)S(1)} collective-permute-done((bf16[144,1024]{1,0:T(8,128)(2,1)S(1)}, bf16[144,1024]{1,0:T(8,128)(2,1)S(1)}, u32[]{:S(2)}, u32[]{:S(2)}) %collective-permute-start.10) | collective-permute-done | bytes 294944 | tf_op jit(solution)/shard_map/ppermute | solution.py:11
  114.4 3.4 collective-permute-done.11
  122.1 3.2 collective-permute-done.8
  127.3 4.0 collective-permute-done.5
  134.8 3.1 collective-permute-done.9
  138.3 3.2 collective-permute-done.6
  143.0 3.7 slice_reduce_fusion.7
  156.3 4.2 collective-permute-done.14
  160.5 3.2 collective-permute-start.17
  166.1 3.7 collective-permute-done.16
  169.8 3.7 collective-permute-start.19
  177.9 3.7 collective-permute-start.21
  185.5 3.9 reshape.135
  189.4 61.3 %all_to_all.20 = bf16[32,36,896]{2,1,0:T(8,128)(2,1)S(1)} all-to-all(bf16[32,36,896]{2,1,0:T(8,128)(2,1)} %reshape.135), channel_id=1, replica_groups=mesh['segment'=8,'y'=4,'z'=8] {'z','y'}, dimensions={0} | all-to-all | bytes 4128768 | tf_op jit(solution)/shard_map/all_to_all | solution.py:115
  253.3 5.0 copy.12
  258.4 4.2 fusion.4
  264.5 3.9 copy.14
  268.4 19.0 %collective-permute-done.22 = bf16[128,7168]{0,1:T(8,128)(2,1)} collective-permute-done((bf16[128,7168]{0,1:T(8,128)(2,1)}, bf16[128,7168]{0,1:T(8,128)(2,1)}, u32[]{:S(2)}, u32[]{:S(2)}) %collective-permute-start.22) | collective-permute-done | bytes 1835040 | tf_op jit(solution)/shard_map/ppermute | solution.py:17
  293.7 60.2 %all_to_all.21 = bf16[32,36,896]{2,1,0:T(8,128)(2,1)} all-to-all(bf16[32,36,896]{2,1,0:T(8,128)(2,1)S(1)} %bitcast.408), channel_id=1, replica_groups=mesh['segment'=8,'y'=4,'z'=8] {'z','y'}, dimensions={0} | all-to-all | bytes 4128768 | tf_op jit(solution)/shard_map/all_to_all | solution.py:59
  353.9 4.0 reshape.141
  369.2 3.3 collective-permute-start.27
  372.5 3.3 collective-permute-done.23
  376.0 3.3 collective-permute-start.34
  382.1 3.4 collective-permute-done.24
  392.3 3.9 collective-permute-done.25
  396.2 3.2 collective-permute-done.31
  400.0 3.3 collective-permute-start.29
  406.0 3.3 collective-permute-done.26
  409.2 3.2 collective-permute-done.32
  414.5 4.7 slice_reduce_fusion.1
  425.5 3.6 collective-permute-done.37
  435.4 5.2 collective-permute-done.39
  440.7 3.2 collective-permute-start.42
  449.3 3.3 collective-permute-start.44
  456.8 3.9 reshape.144
  460.7 6.2 %all-to-all-start.3 = ((bf16[32,36,896]{2,1,0:T(8,128)(2,1)}), bf16[32,36,896]{2,1,0:T(8,128)(2,1)}, u32[]{:S(2)}, u32[]{:S(2)}) async-start(bf16[32,36,896]{2,1,0:T(8,128)(2,1)} %reshape.144), calls=%async_computation.3 | async-start | bytes 4587520 | tf_op jit(solution)/shard_map/all_to_all | solution.py:115
  466.9 4.3 fusion.5
  471.2 41.5 %all-to-all-done.3 = bf16[32,36,896]{2,1,0:T(8,128)(2,1)} async-done(((bf16[32,36,896]{2,1,0:T(8,128)(2,1)}), bf16[32,36,896]{2,1,0:T(8,128)(2,1)}, u32[]{:S(2)}, u32[]{:S(2)}) %all-to-all-start.3) | async-done | bytes 2064416 | tf_op jit(solution)/shard_map/all_to_all | solution.py:115
  512.7 4.2 bitcast_multiply_fusion
  516.9 5.0 copy.16
  527.1 5.9 %copy.17 = bf16[2,1,128,7168]{3,2,1,0:T(8,128)(2,1)} copy(bf16[2,1,128,7168]{2,3,0,1:T(8,128)(2,1)} %maximum_bitcast_fusion) | data formatting | bytes 7340032 | tf_op jit(solution)/shard_map/broadcast_in_dim | solution.py:135
  (169 shorter events, 123.1 us)
Async XLA Ops:
  0.0 155.0 %copy-start = (bf16[1,1,1024,896]{3,2,1,0:T(8,128)(2,1)S(1)}, bf16[1,1,1024,896]{3,2,1,0:T(8,128)(2,1)}, u32[]{:S(2)}) copy-start(bf16[1,1,1024,896]{3,2,1,0:T(8,128)(2,1)} %param.11) | copy-start | bytes 5505028
  18.3 65.9 %all-to-all-start = ((bf16[32,36,896]{2,1,0:T(8,128)(2,1)}), bf16[32,36,896]{2,1,0:T(8,128)(2,1)}, u32[]{:S(2)}, u32[]{:S(2)}) async-start(bf16[32,36,896]{2,1,0:T(8,128)(2,1)} %bitcast.407), calls=%async_computation | async-start | bytes 4587520 | tf_op jit(solution)/shard_map/all_to_all | solution.py:59
  91.3 11.2 %collective-permute-start = (bf16[144,1024]{1,0:T(8,128)(2,1)S(1)}, bf16[144,1024]{1,0:T(8,128)(2,1)S(1)}, u32[]{:S(2)}, u32[]{:S(2)}) collective-permute-start(bf16[144,1024]{1,0:T(8,128)(2,1)S(1)} %get-tuple-element.37), channel_id=1, source_target_pairs={{0,1},{1,2},{2,3},{3,4},{4,5},{5,6},{6,7},{7,0},{8,9},{9,10},{10,1... | collective-permute-start | bytes 884744 | tf_op jit(solution)/shard_map/ppermute | solution.py:11
  94.5 17.3 %collective-permute-start.7 = (bf16[144,1024]{1,0:T(8,128)(2,1)S(1)}, bf16[144,1024]{1,0:T(8,128)(2,1)S(1)}, u32[]{:S(2)}, u32[]{:S(2)}) collective-permute-start(bf16[144,1024]{1,0:T(8,128)(2,1)S(1)} %slice.310), channel_id=1, source_target_pairs={{0,1},{1,2},{2,3},{3,4},{4,5},{5,6},{6,7},{7,0},{8,9},{9,10},{10,1... | collective-permute-start | bytes 884744 | tf_op jit(solution)/shard_map/ppermute | solution.py:11
  98.2 10.0 %collective-permute-start.10 = (bf16[144,1024]{1,0:T(8,128)(2,1)S(1)}, bf16[144,1024]{1,0:T(8,128)(2,1)S(1)}, u32[]{:S(2)}, u32[]{:S(2)}) collective-permute-start(bf16[144,1024]{1,0:T(8,128)(2,1)S(1)} %get-tuple-element.38), channel_id=1, source_target_pairs={{0,7},{1,0},{2,1},{3,2},{4,3},{5,4},{6,5},{7,6},{8,15},{9,8},{10,9... | collective-permute-start | bytes 884744 | tf_op jit(solution)/shard_map/ppermute | solution.py:11
  100.4 14.1 %collective-permute-start.4 = (bf16[144,1024]{1,0:T(8,128)(2,1)S(1)}, bf16[144,1024]{1,0:T(8,128)(2,1)S(1)}, u32[]{:S(2)}, u32[]{:S(2)}) collective-permute-start(bf16[144,1024]{1,0:T(8,128)(2,1)S(1)} %slice.311), channel_id=1, source_target_pairs={{0,7},{1,0},{2,1},{3,2},{4,3},{5,4},{6,5},{7,6},{8,15},{9,8},{10,9... | collective-permute-start | bytes 884744 | tf_op jit(solution)/shard_map/ppermute | solution.py:11
  102.6 9.3 %collective-permute-start.1 = (bf16[144,1024]{1,0:T(8,128)(2,1)S(1)}, bf16[144,1024]{1,0:T(8,128)(2,1)S(1)}, u32[]{:S(2)}, u32[]{:S(2)}) collective-permute-start(bf16[144,1024]{1,0:T(8,128)(2,1)S(1)} %fusion.209), channel_id=1, source_target_pairs={{0,1},{1,2},{2,3},{3,4},{4,5},{5,6},{6,7},{7,0},{8,9},{9,10},{10,1... | collective-permute-start | bytes 884744 | tf_op jit(solution)/shard_map/ppermute | solution.py:11
  108.3 9.5 %collective-permute-start.11 = (bf16[144,1024]{1,0:T(8,128)(2,1)S(1)}, bf16[144,1024]{1,0:T(8,128)(2,1)S(1)}, u32[]{:S(2)}, u32[]{:S(2)}) collective-permute-start(bf16[144,1024]{1,0:T(8,128)(2,1)S(1)} %fusion.201), channel_id=1, source_target_pairs={{0,7},{1,0},{2,1},{3,2},{4,3},{5,4},{6,5},{7,6},{8,15},{9,8},{10,9... | collective-permute-start | bytes 884744 | tf_op jit(solution)/shard_map/ppermute | solution.py:11
  112.0 10.1 %collective-permute-start.2 = (bf16[144,1024]{1,0:T(8,128)(2,1)S(1)}, bf16[144,1024]{1,0:T(8,128)(2,1)S(1)}, u32[]{:S(2)}, u32[]{:S(2)}) collective-permute-start(bf16[144,1024]{1,0:T(8,128)(2,1)S(1)} %get-tuple-element.29), channel_id=1, source_target_pairs={{0,1},{1,2},{2,3},{3,4},{4,5},{5,6},{6,7},{7,0},{8,9},{9,10},{10,1... | collective-permute-start | bytes 884744 | tf_op jit(solution)/shard_map/ppermute | solution.py:11
  112.1 13.2 %collective-permute-start.8 = (bf16[144,1024]{1,0:T(8,128)(2,1)S(1)}, bf16[144,1024]{1,0:T(8,128)(2,1)S(1)}, u32[]{:S(2)}, u32[]{:S(2)}) collective-permute-start(bf16[144,1024]{1,0:T(8,128)(2,1)S(1)} %get-tuple-element.30), channel_id=1, source_target_pairs={{0,1},{1,2},{2,3},{3,4},{4,5},{5,6},{6,7},{7,0},{8,9},{9,10},{10,1... | collective-permute-start | bytes 884744 | tf_op jit(solution)/shard_map/ppermute | solution.py:11
  118.0 9.4 %collective-permute-start.12 = (bf16[144,1024]{1,0:T(8,128)(2,1)S(1)}, bf16[144,1024]{1,0:T(8,128)(2,1)S(1)}, u32[]{:S(2)}, u32[]{:S(2)}) collective-permute-start(bf16[144,1024]{1,0:T(8,128)(2,1)S(1)} %get-tuple-element.34), channel_id=1, source_target_pairs={{0,7},{1,0},{2,1},{3,2},{4,3},{5,4},{6,5},{7,6},{8,15},{9,8},{10,9... | collective-permute-start | bytes 884744 | tf_op jit(solution)/shard_map/ppermute | solution.py:11
  120.2 11.1 %collective-permute-start.5 = (bf16[144,1024]{1,0:T(8,128)(2,1)S(1)}, bf16[144,1024]{1,0:T(8,128)(2,1)S(1)}, u32[]{:S(2)}, u32[]{:S(2)}) collective-permute-start(bf16[144,1024]{1,0:T(8,128)(2,1)S(1)} %get-tuple-element.33), channel_id=1, source_target_pairs={{0,7},{1,0},{2,1},{3,2},{4,3},{5,4},{6,5},{7,6},{8,15},{9,8},{10,9... | collective-permute-start | bytes 884744 | tf_op jit(solution)/shard_map/ppermute | solution.py:11
  125.5 9.3 %collective-permute-start.3 = (bf16[144,1024]{1,0:T(8,128)(2,1)S(1)}, bf16[144,1024]{1,0:T(8,128)(2,1)S(1)}, u32[]{:S(2)}, u32[]{:S(2)}) collective-permute-start(bf16[144,1024]{1,0:T(8,128)(2,1)S(1)} %get-tuple-element.27), channel_id=1, source_target_pairs={{0,1},{1,2},{2,3},{3,4},{4,5},{5,6},{6,7},{7,0},{8,9},{9,10},{10,1... | collective-permute-start | bytes 884744 | tf_op jit(solution)/shard_map/ppermute | solution.py:11
  125.6 12.3 %collective-permute-start.9 = (bf16[144,1024]{1,0:T(8,128)(2,1)S(1)}, bf16[144,1024]{1,0:T(8,128)(2,1)S(1)}, u32[]{:S(2)}, u32[]{:S(2)}) collective-permute-start(bf16[144,1024]{1,0:T(8,128)(2,1)S(1)} %get-tuple-element.28), channel_id=1, source_target_pairs={{0,1},{1,2},{2,3},{3,4},{4,5},{5,6},{6,7},{7,0},{8,9},{9,10},{10,1... | collective-permute-start | bytes 884744 | tf_op jit(solution)/shard_map/ppermute | solution.py:11
  131.5 6.8 %collective-permute-start.13 = (bf16[144,1024]{1,0:T(8,128)(2,1)S(1)}, bf16[144,1024]{1,0:T(8,128)(2,1)S(1)}, u32[]{:S(2)}, u32[]{:S(2)}) collective-permute-start(bf16[144,1024]{1,0:T(8,128)(2,1)S(1)} %get-tuple-element.32), channel_id=1, source_target_pairs={{0,7},{1,0},{2,1},{3,2},{4,3},{5,4},{6,5},{7,6},{8,15},{9,8},{10,9... | collective-permute-start | bytes 884744 | tf_op jit(solution)/shard_map/ppermute | solution.py:11
  133.7 7.8 %collective-permute-start.6 = (bf16[144,1024]{1,0:T(8,128)(2,1)S(1)}, bf16[144,1024]{1,0:T(8,128)(2,1)S(1)}, u32[]{:S(2)}, u32[]{:S(2)}) collective-permute-start(bf16[144,1024]{1,0:T(8,128)(2,1)S(1)} %get-tuple-element.31), channel_id=1, source_target_pairs={{0,7},{1,0},{2,1},{3,2},{4,3},{5,4},{6,5},{7,6},{8,15},{9,8},{10,9... | collective-permute-start | bytes 884744 | tf_op jit(solution)/shard_map/ppermute | solution.py:11
  150.1 10.4 %collective-permute-start.14 = (bf16[144,1024]{1,0:T(8,128)(2,1)S(1)}, bf16[144,1024]{1,0:T(8,128)(2,1)S(1)}, u32[]{:S(2)}, u32[]{:S(2)}) collective-permute-start(bf16[144,1024]{1,0:T(8,128)(2,1)S(1)} %pad_maximum_fusion), channel_id=1, source_target_pairs={{0,1},{1,2},{2,3},{3,4},{4,5},{5,6},{6,7},{7,0},{8,9},{9,10},{10,1... | collective-permute-start | bytes 884744 | tf_op jit(solution)/shard_map/ppermute | solution.py:11
  150.7 9.8 %collective-permute-start.15 = (bf16[144,1024]{1,0:T(8,128)(2,1)S(1)}, bf16[144,1024]{1,0:T(8,128)(2,1)S(1)}, u32[]{:S(2)}, u32[]{:S(2)}) collective-permute-start(bf16[144,1024]{1,0:T(8,128)(2,1)S(1)} %pad_maximum_fusion), channel_id=1, source_target_pairs={{0,7},{1,0},{2,1},{3,2},{4,3},{5,4},{6,5},{7,6},{8,15},{9,8},{10,9... | collective-permute-start | bytes 884744 | tf_op jit(solution)/shard_map/ppermute | solution.py:11
  160.5 9.4 %collective-permute-start.16 = (bf16[144,1024]{1,0:T(8,128)(2,1)S(1)}, bf16[144,1024]{1,0:T(8,128)(2,1)S(1)}, u32[]{:S(2)}, u32[]{:S(2)}) collective-permute-start(bf16[144,1024]{1,0:T(8,128)(2,1)S(1)} %collective-permute-done.14), channel_id=1, source_target_pairs={{0,1},{1,2},{2,3},{3,4},{4,5},{5,6},{6,7},{7,0},{8,9},{9,10},{10,1... | collective-permute-start | bytes 884744 | tf_op jit(solution)/shard_map/ppermute | solution.py:11
  160.5 9.4 %collective-permute-start.17 = (bf16[144,1024]{1,0:T(8,128)(2,1)S(1)}, bf16[144,1024]{1,0:T(8,128)(2,1)S(1)}, u32[]{:S(2)}, u32[]{:S(2)}) collective-permute-start(bf16[144,1024]{1,0:T(8,128)(2,1)S(1)} %collective-permute-done.15), channel_id=1, source_target_pairs={{0,7},{1,0},{2,1},{3,2},{4,3},{5,4},{6,5},{7,6},{8,15},{9,8},{10,9... | collective-permute-start | bytes 884744 | tf_op jit(solution)/shard_map/ppermute | solution.py:11
  169.8 7.9 %collective-permute-start.18 = (bf16[144,1024]{1,0:T(8,128)(2,1)S(1)}, bf16[144,1024]{1,0:T(8,128)(2,1)S(1)}, u32[]{:S(2)}, u32[]{:S(2)}) collective-permute-start(bf16[144,1024]{1,0:T(8,128)(2,1)S(1)} %collective-permute-done.16), channel_id=1, source_target_pairs={{0,1},{1,2},{2,3},{3,4},{4,5},{5,6},{6,7},{7,0},{8,9},{9,10},{10,1... | collective-permute-start | bytes 884744 | tf_op jit(solution)/shard_map/ppermute | solution.py:11
  169.8 8.0 %collective-permute-start.19 = (bf16[144,1024]{1,0:T(8,128)(2,1)S(1)}, bf16[144,1024]{1,0:T(8,128)(2,1)S(1)}, u32[]{:S(2)}, u32[]{:S(2)}) collective-permute-start(bf16[144,1024]{1,0:T(8,128)(2,1)S(1)} %collective-permute-done.17), channel_id=1, source_target_pairs={{0,7},{1,0},{2,1},{3,2},{4,3},{5,4},{6,5},{7,6},{8,15},{9,8},{10,9... | collective-permute-start | bytes 884744 | tf_op jit(solution)/shard_map/ppermute | solution.py:11
  177.8 6.4 %collective-permute-start.20 = (bf16[144,512]{1,0:T(8,128)(2,1)S(1)}, bf16[144,512]{1,0:T(8,128)(2,1)S(1)}, u32[]{:S(2)}, u32[]{:S(2)}) collective-permute-start(bf16[144,512]{1,0:T(8,128)(2,1)S(1)} %slice.200), channel_id=1, source_target_pairs={{0,1},{1,2},{2,3},{3,4},{4,5},{5,6},{6,7},{7,0},{8,9},{9,10},{10,1... | collective-permute-start | bytes 442376 | tf_op jit(solution)/shard_map/ppermute | solution.py:11
  177.9 6.4 %collective-permute-start.21 = (bf16[144,512]{1,0:T(8,128)(2,1)S(1)}, bf16[144,512]{1,0:T(8,128)(2,1)S(1)}, u32[]{:S(2)}, u32[]{:S(2)}) collective-permute-start(bf16[144,512]{1,0:T(8,128)(2,1)S(1)} %slice.201), channel_id=1, source_target_pairs={{0,7},{1,0},{2,1},{3,2},{4,3},{5,4},{6,5},{7,6},{8,15},{9,8},{10,9... | collective-permute-start | bytes 442376 | tf_op jit(solution)/shard_map/ppermute | solution.py:11
  262.6 24.8 %collective-permute-start.22 = (bf16[128,7168]{0,1:T(8,128)(2,1)}, bf16[128,7168]{0,1:T(8,128)(2,1)}, u32[]{:S(2)}, u32[]{:S(2)}) collective-permute-start(bf16[128,7168]{0,1:T(8,128)(2,1)} %fusion.4), channel_id=1, source_target_pairs={{0,32},{32,64},{64,96},{96,128},{128,160},{160,192},{192,224},{1,3... | collective-permute-start | bytes 5505032 | tf_op jit(solution)/shard_map/ppermute | solution.py:17
  364.8 10.9 %collective-permute-start.23 = (bf16[144,1024]{1,0:T(8,128)(2,1)S(1)}, bf16[144,1024]{1,0:T(8,128)(2,1)S(1)}, u32[]{:S(2)}, u32[]{:S(2)}) collective-permute-start(bf16[144,1024]{1,0:T(8,128)(2,1)S(1)} %get-tuple-element.35), channel_id=1, source_target_pairs={{0,1},{1,2},{2,3},{3,4},{4,5},{5,6},{6,7},{7,0},{8,9},{9,10},{10,1... | collective-permute-start | bytes 884744 | tf_op jit(solution)/shard_map/ppermute | solution.py:11
  365.7 10.2 %collective-permute-start.33 = (bf16[144,1024]{1,0:T(8,128)(2,1)S(1)}, bf16[144,1024]{1,0:T(8,128)(2,1)S(1)}, u32[]{:S(2)}, u32[]{:S(2)}) collective-permute-start(bf16[144,1024]{1,0:T(8,128)(2,1)S(1)} %get-tuple-element.36), channel_id=1, source_target_pairs={{0,7},{1,0},{2,1},{3,2},{4,3},{5,4},{6,5},{7,6},{8,15},{9,8},{10,9... | collective-permute-start | bytes 884744 | tf_op jit(solution)/shard_map/ppermute | solution.py:11
  369.0 13.0 %collective-permute-start.30 = (bf16[144,1024]{1,0:T(8,128)(2,1)S(1)}, bf16[144,1024]{1,0:T(8,128)(2,1)S(1)}, u32[]{:S(2)}, u32[]{:S(2)}) collective-permute-start(bf16[144,1024]{1,0:T(8,128)(2,1)S(1)} %slice.308), channel_id=1, source_target_pairs={{0,1},{1,2},{2,3},{3,4},{4,5},{5,6},{6,7},{7,0},{8,9},{9,10},{10,1... | collective-permute-start | bytes 884744 | tf_op jit(solution)/shard_map/ppermute | solution.py:11
  369.2 17.1 %collective-permute-start.27 = (bf16[144,1024]{1,0:T(8,128)(2,1)S(1)}, bf16[144,1024]{1,0:T(8,128)(2,1)S(1)}, u32[]{:S(2)}, u32[]{:S(2)}) collective-permute-start(bf16[144,1024]{1,0:T(8,128)(2,1)S(1)} %slice.309), channel_id=1, source_target_pairs={{0,7},{1,0},{2,1},{3,2},{4,3},{5,4},{6,5},{7,6},{8,15},{9,8},{10,9... | collective-permute-start | bytes 884744 | tf_op jit(solution)/shard_map/ppermute | solution.py:11
  375.8 9.7 %collective-permute-start.24 = (bf16[144,1024]{1,0:T(8,128)(2,1)S(1)}, bf16[144,1024]{1,0:T(8,128)(2,1)S(1)}, u32[]{:S(2)}, u32[]{:S(2)}) collective-permute-start(bf16[144,1024]{1,0:T(8,128)(2,1)S(1)} %fusion.197), channel_id=1, source_target_pairs={{0,1},{1,2},{2,3},{3,4},{4,5},{5,6},{6,7},{7,0},{8,9},{9,10},{10,1... | collective-permute-start | bytes 884744 | tf_op jit(solution)/shard_map/ppermute | solution.py:11
  376.0 10.3 %collective-permute-start.34 = (bf16[144,1024]{1,0:T(8,128)(2,1)S(1)}, bf16[144,1024]{1,0:T(8,128)(2,1)S(1)}, u32[]{:S(2)}, u32[]{:S(2)}) collective-permute-start(bf16[144,1024]{1,0:T(8,128)(2,1)S(1)} %fusion.189), channel_id=1, source_target_pairs={{0,7},{1,0},{2,1},{3,2},{4,3},{5,4},{6,5},{7,6},{8,15},{9,8},{10,9... | collective-permute-start | bytes 884744 | tf_op jit(solution)/shard_map/ppermute | solution.py:11
  385.7 10.6 %collective-permute-start.25 = (bf16[144,1024]{1,0:T(8,128)(2,1)S(1)}, bf16[144,1024]{1,0:T(8,128)(2,1)S(1)}, u32[]{:S(2)}, u32[]{:S(2)}) collective-permute-start(bf16[144,1024]{1,0:T(8,128)(2,1)S(1)} %get-tuple-element.19), channel_id=1, source_target_pairs={{0,1},{1,2},{2,3},{3,4},{4,5},{5,6},{6,7},{7,0},{8,9},{9,10},{10,1... | collective-permute-start | bytes 884744 | tf_op jit(solution)/shard_map/ppermute | solution.py:11
  385.8 13.6 %collective-permute-start.31 = (bf16[144,1024]{1,0:T(8,128)(2,1)S(1)}, bf16[144,1024]{1,0:T(8,128)(2,1)S(1)}, u32[]{:S(2)}, u32[]{:S(2)}) collective-permute-start(bf16[144,1024]{1,0:T(8,128)(2,1)S(1)} %get-tuple-element.20), channel_id=1, source_target_pairs={{0,1},{1,2},{2,3},{3,4},{4,5},{5,6},{6,7},{7,0},{8,9},{9,10},{10,1... | collective-permute-start | bytes 884744 | tf_op jit(solution)/shard_map/ppermute | solution.py:11
  386.5 13.3 %collective-permute-start.28 = (bf16[144,1024]{1,0:T(8,128)(2,1)S(1)}, bf16[144,1024]{1,0:T(8,128)(2,1)S(1)}, u32[]{:S(2)}, u32[]{:S(2)}) collective-permute-start(bf16[144,1024]{1,0:T(8,128)(2,1)S(1)} %get-tuple-element.23), channel_id=1, source_target_pairs={{0,7},{1,0},{2,1},{3,2},{4,3},{5,4},{6,5},{7,6},{8,15},{9,8},{10,9... | collective-permute-start | bytes 884744 | tf_op jit(solution)/shard_map/ppermute | solution.py:11
  389.4 10.4 %collective-permute-start.35 = (bf16[144,1024]{1,0:T(8,128)(2,1)S(1)}, bf16[144,1024]{1,0:T(8,128)(2,1)S(1)}, u32[]{:S(2)}, u32[]{:S(2)}) collective-permute-start(bf16[144,1024]{1,0:T(8,128)(2,1)S(1)} %get-tuple-element.24), channel_id=1, source_target_pairs={{0,7},{1,0},{2,1},{3,2},{4,3},{5,4},{6,5},{7,6},{8,15},{9,8},{10,9... | collective-permute-start | bytes 884744 | tf_op jit(solution)/shard_map/ppermute | solution.py:11
  399.6 9.6 %collective-permute-start.26 = (bf16[144,1024]{1,0:T(8,128)(2,1)S(1)}, bf16[144,1024]{1,0:T(8,128)(2,1)S(1)}, u32[]{:S(2)}, u32[]{:S(2)}) collective-permute-start(bf16[144,1024]{1,0:T(8,128)(2,1)S(1)} %get-tuple-element.17), channel_id=1, source_target_pairs={{0,1},{1,2},{2,3},{3,4},{4,5},{5,6},{6,7},{7,0},{8,9},{9,10},{10,1... | collective-permute-start | bytes 884744 | tf_op jit(solution)/shard_map/ppermute | solution.py:11
  399.7 12.7 %collective-permute-start.32 = (bf16[144,1024]{1,0:T(8,128)(2,1)S(1)}, bf16[144,1024]{1,0:T(8,128)(2,1)S(1)}, u32[]{:S(2)}, u32[]{:S(2)}) collective-permute-start(bf16[144,1024]{1,0:T(8,128)(2,1)S(1)} %get-tuple-element.18), channel_id=1, source_target_pairs={{0,1},{1,2},{2,3},{3,4},{4,5},{5,6},{6,7},{7,0},{8,9},{9,10},{10,1... | collective-permute-start | bytes 884744 | tf_op jit(solution)/shard_map/ppermute | solution.py:11
  400.0 12.4 %collective-permute-start.29 = (bf16[144,1024]{1,0:T(8,128)(2,1)S(1)}, bf16[144,1024]{1,0:T(8,128)(2,1)S(1)}, u32[]{:S(2)}, u32[]{:S(2)}) collective-permute-start(bf16[144,1024]{1,0:T(8,128)(2,1)S(1)} %get-tuple-element.21), channel_id=1, source_target_pairs={{0,7},{1,0},{2,1},{3,2},{4,3},{5,4},{6,5},{7,6},{8,15},{9,8},{10,9... | collective-permute-start | bytes 884744 | tf_op jit(solution)/shard_map/ppermute | solution.py:11
  403.3 9.1 %collective-permute-start.36 = (bf16[144,1024]{1,0:T(8,128)(2,1)S(1)}, bf16[144,1024]{1,0:T(8,128)(2,1)S(1)}, u32[]{:S(2)}, u32[]{:S(2)}) collective-permute-start(bf16[144,1024]{1,0:T(8,128)(2,1)S(1)} %get-tuple-element.22), channel_id=1, source_target_pairs={{0,7},{1,0},{2,1},{3,2},{4,3},{5,4},{6,5},{7,6},{8,15},{9,8},{10,9... | collective-permute-start | bytes 884744 | tf_op jit(solution)/shard_map/ppermute | solution.py:11
  419.4 9.8 %collective-permute-start.37 = (bf16[144,1024]{1,0:T(8,128)(2,1)S(1)}, bf16[144,1024]{1,0:T(8,128)(2,1)S(1)}, u32[]{:S(2)}, u32[]{:S(2)}) collective-permute-start(bf16[144,1024]{1,0:T(8,128)(2,1)S(1)} %pad_maximum_fusion.1), channel_id=1, source_target_pairs={{0,1},{1,2},{2,3},{3,4},{4,5},{5,6},{6,7},{7,0},{8,9},{9,10},{10,1... | collective-permute-start | bytes 884744 | tf_op jit(solution)/shard_map/ppermute | solution.py:11
  421.8 9.5 %collective-permute-start.38 = (bf16[144,1024]{1,0:T(8,128)(2,1)S(1)}, bf16[144,1024]{1,0:T(8,128)(2,1)S(1)}, u32[]{:S(2)}, u32[]{:S(2)}) collective-permute-start(bf16[144,1024]{1,0:T(8,128)(2,1)S(1)} %pad_maximum_fusion.1), channel_id=1, source_target_pairs={{0,7},{1,0},{2,1},{3,2},{4,3},{5,4},{6,5},{7,6},{8,15},{9,8},{10,9... | collective-permute-start | bytes 884744 | tf_op jit(solution)/shard_map/ppermute | solution.py:11
  429.2 11.4 %collective-permute-start.39 = (bf16[144,1024]{1,0:T(8,128)(2,1)S(1)}, bf16[144,1024]{1,0:T(8,128)(2,1)S(1)}, u32[]{:S(2)}, u32[]{:S(2)}) collective-permute-start(bf16[144,1024]{1,0:T(8,128)(2,1)S(1)} %collective-permute-done.37), channel_id=1, source_target_pairs={{0,1},{1,2},{2,3},{3,4},{4,5},{5,6},{6,7},{7,0},{8,9},{9,10},{10,1... | collective-permute-start | bytes 884744 | tf_op jit(solution)/shard_map/ppermute | solution.py:11
  431.3 9.4 %collective-permute-start.40 = (bf16[144,1024]{1,0:T(8,128)(2,1)S(1)}, bf16[144,1024]{1,0:T(8,128)(2,1)S(1)}, u32[]{:S(2)}, u32[]{:S(2)}) collective-permute-start(bf16[144,1024]{1,0:T(8,128)(2,1)S(1)} %collective-permute-done.38), channel_id=1, source_target_pairs={{0,7},{1,0},{2,1},{3,2},{4,3},{5,4},{6,5},{7,6},{8,15},{9,8},{10,9... | collective-permute-start | bytes 884744 | tf_op jit(solution)/shard_map/ppermute | solution.py:11
  440.6 8.5 %collective-permute-start.41 = (bf16[144,1024]{1,0:T(8,128)(2,1)S(1)}, bf16[144,1024]{1,0:T(8,128)(2,1)S(1)}, u32[]{:S(2)}, u32[]{:S(2)}) collective-permute-start(bf16[144,1024]{1,0:T(8,128)(2,1)S(1)} %collective-permute-done.39), channel_id=1, source_target_pairs={{0,1},{1,2},{2,3},{3,4},{4,5},{5,6},{6,7},{7,0},{8,9},{9,10},{10,1... | collective-permute-start | bytes 884744 | tf_op jit(solution)/shard_map/ppermute | solution.py:11
  440.7 8.5 %collective-permute-start.42 = (bf16[144,1024]{1,0:T(8,128)(2,1)S(1)}, bf16[144,1024]{1,0:T(8,128)(2,1)S(1)}, u32[]{:S(2)}, u32[]{:S(2)}) collective-permute-start(bf16[144,1024]{1,0:T(8,128)(2,1)S(1)} %collective-permute-done.40), channel_id=1, source_target_pairs={{0,7},{1,0},{2,1},{3,2},{4,3},{5,4},{6,5},{7,6},{8,15},{9,8},{10,9... | collective-permute-start | bytes 884744 | tf_op jit(solution)/shard_map/ppermute | solution.py:11
  449.1 6.4 %collective-permute-start.43 = (bf16[144,512]{1,0:T(8,128)(2,1)S(1)}, bf16[144,512]{1,0:T(8,128)(2,1)S(1)}, u32[]{:S(2)}, u32[]{:S(2)}) collective-permute-start(bf16[144,512]{1,0:T(8,128)(2,1)S(1)} %slice.222), channel_id=1, source_target_pairs={{0,1},{1,2},{2,3},{3,4},{4,5},{5,6},{6,7},{7,0},{8,9},{9,10},{10,1... | collective-permute-start | bytes 442376 | tf_op jit(solution)/shard_map/ppermute | solution.py:11
  449.3 6.3 %collective-permute-start.44 = (bf16[144,512]{1,0:T(8,128)(2,1)S(1)}, bf16[144,512]{1,0:T(8,128)(2,1)S(1)}, u32[]{:S(2)}, u32[]{:S(2)}) collective-permute-start(bf16[144,512]{1,0:T(8,128)(2,1)S(1)} %slice.223), channel_id=1, source_target_pairs={{0,7},{1,0},{2,1},{3,2},{4,3},{5,4},{6,5},{7,6},{8,15},{9,8},{10,9... | collective-permute-start | bytes 442376 | tf_op jit(solution)/shard_map/ppermute | solution.py:11
  460.7 51.9 %all-to-all-start.3 = ((bf16[32,36,896]{2,1,0:T(8,128)(2,1)}), bf16[32,36,896]{2,1,0:T(8,128)(2,1)}, u32[]{:S(2)}, u32[]{:S(2)}) async-start(bf16[32,36,896]{2,1,0:T(8,128)(2,1)} %reshape.144), calls=%async_computation.3 | async-start | bytes 4587520 | tf_op jit(solution)/shard_map/all_to_all | solution.py:115
  (8 other events, 87.8 us)

commit v2 on v1

v2 whole, which is shorter than its diff:
```python
import functools

import jax
import jax.numpy as jnp
from jax import lax
from jax.experimental import pallas as pl
from jax.experimental.pallas import tpu as pltpu
from jax.sharding import Mesh, PartitionSpec as P

EPSILON = 1e-06
TILE = 16
VMEM_BYTES = 40 * 2**20
SENT = ((4,), (5, 3), (6, 2, 7, 1, 0))
GIVEN = ((0, 1, 7, 2, 6), (3, 5), (4,))


def shifted(value, axis, by):
    count = lax.axis_size(axis)
    return lax.ppermute(value, axis, [(i, (i + by) % count) for i in range(count)])


def passed_along(shard, axis, by):
    count = lax.axis_size(axis)
    pairs = [(i, i + by) for i in range(count) if 0 <= i + by < count]
    return lax.ppermute(shard, axis, pairs)


def local_call(body, out_shape, operands, flops, scalars=0):
    vmem = pl.BlockSpec(memory_space=pltpu.VMEM)
    smem = pl.BlockSpec(memory_space=pltpu.SMEM)
    moved = sum(v.size * v.dtype.itemsize for v in (*operands, *jax.tree.leaves(out_shape)))
    return pl.pallas_call(
        body,
        out_shape=out_shape,
        in_specs=[smem] * scalars + [vmem] * (len(operands) - scalars),
        out_specs=jax.tree.map(lambda _: vmem, out_shape),
        compiler_params=pltpu.CompilerParams(vmem_limit_bytes=VMEM_BYTES),
        cost_estimate=pl.CostEstimate(flops=flops, bytes_accessed=moved, transcendentals=0),
    )(*operands)


def columns(index, width):
    return pl.ds(pl.multiple_of(index * width, 128), width)


def stream_piece(info, streams, cols):
    if len(streams) == 1:
        return streams[0][:, cols].astype(jnp.float32)
    first = (jnp.zeros((1, 1), jnp.int32) + info[1]) == 0
    return jnp.where(
        first, streams[0][:, cols].astype(jnp.float32), streams[1][:, cols].astype(jnp.float32)
    )


def sending_body(split, groups, n_streams, info, *refs):
    streams, (gain, pick), outs = refs[:n_streams], refs[n_streams : n_streams + 2], refs[n_streams + 2 :]
    width = gain.shape[1] // split
    squares = 0.0
    for piece in range(split):
        values = stream_piece(info, streams, pl.ds(piece * width, width))
        squares = squares + jnp.sum(values * values, axis=1, keepdims=True)
    scale = lax.rsqrt(squares / gain.shape[1] + EPSILON)
    block_rows = pick.shape[0] // groups
    for number, offsets in enumerate(SENT):
        for spot, offset in enumerate(offsets):
            cols = columns(lax.rem(info[0] + offset, split), width)
            normed = (stream_piece(info, streams, cols) * scale * gain[:, cols]).astype(jnp.bfloat16)
            rows = jnp.dot(pick[...], normed, preferred_element_type=jnp.float32)
            rows = rows.astype(jnp.bfloat16)
            for ahead in range(groups):
                outs[number * groups + ahead][spot] = rows[
                    ahead * block_rows : (ahead + 1) * block_rows
                ]


def gathered_body(groups, main, *refs):
    ins, outs = refs[:groups], refs[groups:]
    for spot, out in enumerate(outs):
        rest = ins[0][spot, main:].astype(jnp.float32)
        for ahead in range(groups):
            out[ahead * main : (ahead + 1) * main] = ins[ahead][spot, :main]
            if ahead:
                rest = rest + ins[ahead][spot, main:].astype(jnp.float32)
        out[groups * main :] = rest.astype(jnp.bfloat16)


def spread_body(groups, main, count, *refs):
    ins, outs = refs[:count], refs[count:]
    for spot in range(count):
        for ahead in range(groups):
            outs[ahead][spot, :main] = ins[spot][ahead * main : (ahead + 1) * main]
            outs[ahead][spot, main:] = ins[spot][groups * main :]


def hidden_body(own, low_up, low_down, high_up, high_down, out):
    half = low_up.shape[1]
    for part, (up, down) in enumerate(((low_up, low_down), (high_up, high_down))):
        for block in range(half // 256):
            at = block * 256
            sums = (
                own[:, part * half + at : part * half + at + 256]
                + up[:, at : at + 256].astype(jnp.float32)
                + down[:, at : at + 256].astype(jnp.float32)
            )
            gate, raised = sums[:, :128], sums[:, 128:]
            to = (part * half + at) // 2
            out[:, to : to + 128] = (gate / (1.0 + jnp.exp(-gate)) * raised).astype(jnp.bfloat16)


def combining_body(split, groups, n_streams, n_before, info, *refs):
    streams, (place_back, weight) = refs[:n_streams], refs[n_streams : n_streams + 2]
    before = refs[n_streams + 2 : n_streams + 2 + n_before]
    blocks, out = refs[n_streams + 2 + n_before : -1], refs[-1]
    width = out.shape[-1] // split
    if n_before:
        out[0] = before[0][...]
    for number, offsets in enumerate(GIVEN):
        for spot, offset in enumerate(offsets):
            cols = columns(lax.rem(info[0] + (split - offset), split), width)
            rows = jnp.concatenate(
                [blocks[number * groups + ahead][spot] for ahead in range(groups)], axis=0
            )
            chosen = jnp.dot(place_back[...], rows, preferred_element_type=jnp.float32)
            value = (stream_piece(info, streams, cols) + chosen * weight[...]).astype(jnp.bfloat16)
            if n_before:
                out[1, :, cols] = value
            else:
                out[:, cols] = value


def per_device(tokens, entering, norm_gain, gate_up, down_proj, expert_ids, gate_weights):
    split = lax.axis_size("z")
    groups = lax.axis_size("y")
    row, place = lax.axis_index("y"), lax.axis_index("z")
    info = jnp.stack([place, lax.axis_index("segment")]).astype(jnp.int32)
    tok_rows, model_width = entering.shape
    slot_cap = 9 * tok_rows // (8 * groups)
    main = slot_cap // TILE * TILE
    rest = slot_cap - main
    block_rows = main + groups * rest
    chunk_rows = groups * slot_cap
    piece_width = model_width // split
    hidden_width = down_proj.shape[2]
    half = hidden_width
    far = split // 2
    bf16 = jnp.bfloat16

    flat_ids = expert_ids[0].reshape(tok_rows)
    member = (flat_ids[:, None] == jnp.arange(groups, dtype=jnp.int32)[None, :]).astype(jnp.int32)
    slot_of = jnp.sum((jnp.cumsum(member, axis=0) - 1) * member, axis=1)
    in_block = jnp.where(slot_of < main, slot_of, slot_of + row * rest)
    target = (flat_ids - row + groups) % groups * block_rows + in_block
    all_rows = jnp.arange(groups * block_rows, dtype=jnp.int32)
    pick = (all_rows[:, None] == target[None, :]).astype(bf16)
    place_back = (target[:, None] == all_rows[None, :]).astype(bf16)
    token_weight = gate_weights[0]
    gain = norm_gain
    weights_in = gate_up[0, 0].reshape(piece_width, 2 * hidden_width)
    weights_out = down_proj[0, 0]
    pick_flops = 2 * groups * block_rows * tok_rows * model_width

    def moe_layer(streams, before):
        sent = local_call(
            functools.partial(sending_body, split, groups, len(streams)),
            [
                jax.ShapeDtypeStruct((len(offsets), block_rows, piece_width), bf16)
                for offsets in SENT
                for _ in range(groups)
            ],
            (info, *streams, gain, pick),
            pick_flops,
            1,
        )
        arrived = {}
        for number, offsets in enumerate(SENT):
            blocks = [
                shifted(sent[number * groups + ahead], "y", ahead) if ahead else sent[number * groups]
                for ahead in range(groups)
            ]
            whole = local_call(
                functools.partial(gathered_body, groups, main),
                [jax.ShapeDtypeStruct((chunk_rows, piece_width), bf16) for _ in offsets],
                blocks,
                0,
            )
            for offset, rows in zip(offsets, whole):
                arrived[-offset % split] = shifted(rows, "z", offset) if offset else rows

        def partial_sums(offset):
            return jnp.dot(arrived[offset % split], weights_in, preferred_element_type=jnp.float32)

        opposite = partial_sums(far).astype(bf16)
        low_up, high_down = opposite[:, :half], opposite[:, half:]
        high_up = low_down = None
        for step in range(far - 1, 0, -1):
            low_up = shifted(low_up, "z", 1)
            high_down = shifted(high_down, "z", -1)
            if high_up is not None:
                high_up = shifted(high_up, "z", 1)
                low_down = shifted(low_down, "z", -1)
            ahead, behind = partial_sums(step), partial_sums(-step)
            low_up = (low_up.astype(jnp.float32) + ahead[:, :half]).astype(bf16)
            high_down = (high_down.astype(jnp.float32) + behind[:, half:]).astype(bf16)
            if high_up is None:
                high_up = ahead[:, half:].astype(bf16)
                low_down = behind[:, :half].astype(bf16)
            else:
                high_up = (high_up.astype(jnp.float32) + ahead[:, half:]).astype(bf16)
                low_down = (low_down.astype(jnp.float32) + behind[:, :half]).astype(bf16)
        low_up, high_up = shifted(low_up, "z", 1), shifted(high_up, "z", 1)
        low_down, high_down = shifted(low_down, "z", -1), shifted(high_down, "z", -1)
        hidden = local_call(
            hidden_body,
            jax.ShapeDtypeStruct((chunk_rows, hidden_width), bf16),
            (partial_sums(0), low_up, low_down, high_up, high_down),
            8 * chunk_rows * hidden_width,
        )

        home = {}

        def projected(rows, offset):
            block = jnp.dot(rows, weights_out, preferred_element_type=jnp.float32).astype(bf16)
            home[offset % split] = shifted(block, "z", offset) if offset else block

        from_below = from_above = hidden
        projected(hidden, 0)
        for step in range(1, far):
            from_below = shifted(from_below, "z", 1)
            from_above = shifted(from_above, "z", -1)
            projected(from_below, -step)
            projected(from_above, step)
        left = shifted(from_below[:, : half // 2], "z", 1)
        right = shifted(from_above[:, half // 2 :], "z", -1)
        projected(jnp.concatenate([left, right], axis=1), far)

        returned = []
        for offsets in GIVEN:
            parts = local_call(
                functools.partial(spread_body, groups, main, len(offsets)),
                [
                    jax.ShapeDtypeStruct((len(offsets), block_rows, piece_width), bf16)
                    for _ in range(groups)
                ],
                [home[offset] for offset in offsets],
                0,
            )
            returned += [
                shifted(part, "y", -ahead) if ahead else part for ahead, part in enumerate(parts)
            ]
        return local_call(
            functools.partial(combining_body, split, groups, len(streams), len(before)),
            jax.ShapeDtypeStruct((2,) * len(before) + (tok_rows, model_width), bf16),
            (info, *streams, place_back, token_weight, *before, *returned),
            pick_flops,
            1,
        )

    first_result = moe_layer((tokens[0],), ())
    passed = passed_along(first_result, "segment", 1)
    both_results = moe_layer((entering, passed), (first_result,))
    return both_results[:, None]


def solution(mesh):
    segments, experts = mesh.devices.shape
    split = 8
    fine = Mesh(mesh.devices.reshape(segments, experts // split, split), ("segment", "y", "z"))
    both = ("y", "z")
    in_specs = (
        P("segment", both, None),
        P(both, None),
        P("segment", None),
        P("segment", both, None, None, None, None),
        P("segment", both, None, None),
        P("segment", both, None),
        P("segment", both, None),
    )
    out_specs = P(None, "segment", both, None)
    return jax.shard_map(
        per_device, mesh=fine, in_specs=in_specs, out_specs=out_specs, check_vma=False
    )
```

time: 544 us -> 485 us (0.89)
  the two profiles are of different devices: /device:TPU:2 before, /device:TPU:4 now
where the time goes in v2:
time: 485 us; the launch traced here: 476 us
  waiting for transfers between devices  231 us (48%)
  starting transfers between devices  184 us (38%)
  matrix products  23 us (5%)
  local copies, waits for them, and re-layouts  17 us (4%)
  Pallas kernels  14.2 us (3%)
    ppermute x108, waiting for transfers between devices, shifted(): lax.ppermute(value, axis, [(i, (i + by) % count) for i in range(count)])  209 us
    ppermute x108, starting transfers between devices, shifted(): lax.ppermute(value, axis, [(i, (i + by) % count) for i in range(count)])  182 us
    ppermute x1, waiting for transfers between devices, passed_along(): return lax.ppermute(shard, axis, pairs)  22.6 us
    dot_general x16, matrix products, partial_sums(): jnp.dot(arrived[offset % split], weights_in, preferred_element_type=jnp.f...  15.1 us
    pallas_call x18, Pallas kernels, local_call(): pl.pallas_call(body, out_shape=out_shape, in_specs=[smem] * scalars + [vm...  14.2 us
  transfers between devices with their start and end apart: 109, of which 57 were waited for; matrix products, arithmetic and copies ran while one was open for 7% of the time, Pallas kernels for 1%

profile of v2, /device:TPU:4, one launch (start us, length us, event | category | flops | bytes accessed | tf_op | source)
XLA Modules:
  0.0 475.6 jit_solution(9445189174267034847)
XLA Ops:
  17.3 7.3 %collective-permute-start.6 = (bf16[144,896]{1,0:T(8,128)(2,1)S(1)}, bf16[144,896]{1,0:T(8,128)(2,1)}, u32[]{:S(2)}, u32[]{:S(2)}) collective-permute-start(bf16[144,896]{1,0:T(8,128)(2,1)S(1)} %shard_map.75), channel_id=1, source_target_pairs={{0,4},{1,5},{2,6},{3,7},{4,0},{5,1},{6,2},{7,3},{8,12},{9,13},{10,... | collective-permute-start | bytes 774152 | tf_op jit(solution)/shard_map/ppermute | solution.py:19
  31.2 7.1 %reshape_squeeze.7 = bf16[896,2048]{1,0:T(8,128)(2,1)} reshape(bf16[1,1,896,8,2,128]{5,4,3,2,1,0:T(2,128)(2,1)} %param.10) | data formatting | bytes 7340032 | tf_op jit(solution)/shard_map/reshape;squeeze | solution.py:158
  50.4 4.5 collective-permute-done.refs_1_
  65.8 4.6 collective-permute-done.26
  72.9 6.0 %collective-permute-done.19 = bf16[144,896]{1,0:T(8,128)(2,1)S(1)} collective-permute-done((bf16[144,896]{1,0:T(8,128)(2,1)S(1)}, bf16[144,896]{1,0:T(8,128)(2,1)S(1)}, u32[]{:S(2)}, u32[]{:S(2)}) %collective-permute-start.19) | collective-permute-done | bytes 258080 | tf_op jit(solution)/shard_map/ppermute | solution.py:19
  79.7 4.1 collective-permute-done.21
  88.1 9.2 %collective-permute-done.27 = bf16[144,1024]{1,0:T(8,128)(2,1)S(1)} collective-permute-done((bf16[144,1024]{1,0:T(8,128)(2,1)S(1)}, bf16[144,1024]{1,0:T(8,128)(2,1)S(1)}, u32[]{:S(2)}, u32[]{:S(2)}) %collective-permute-start.27) | collective-permute-done | bytes 294944 | tf_op jit(solution)/shard_map/ppermute | solution.py:19
  103.4 4.1 collective-permute-done.20
  107.5 4.6 collective-permute-done.28
  112.4 3.8 collective-permute-start.22
  119.3 4.3 collective-permute-done.22.low_down
  123.6 3.8 collective-permute-done.29.high_down
  127.6 3.5 collective-permute-done.25.high_up
  133.5 5.9 %collective-permute-done.30 = bf16[144,1024]{1,0:T(8,128)(2,1)S(1)} collective-permute-done((bf16[144,1024]{1,0:T(8,128)(2,1)S(1)}, bf16[144,1024]{1,0:T(8,128)(2,1)S(1)}, u32[]{:S(2)}, u32[]{:S(2)}) %collective-permute-start.30) | collective-permute-done | bytes 294944 | tf_op jit(solution)/shard_map/ppermute | solution.py:19
  145.9 3.5 collective-permute-done.34
  150.4 3.4 collective-permute-start.41
  153.8 6.7 %collective-permute-done.36 = bf16[144,1024]{1,0:T(8,128)(2,1)S(1)} collective-permute-done((bf16[144,1024]{1,0:T(8,128)(2,1)S(1)}, bf16[144,1024]{1,0:T(8,128)(2,1)S(1)}, u32[]{:S(2)}, u32[]{:S(2)}) %collective-permute-start.36) | collective-permute-done | bytes 294944 | tf_op jit(solution)/shard_map/ppermute | solution.py:19
  164.6 6.7 %collective-permute-done.37.refs_4_ = bf16[144,896]{1,0:T(8,128)(2,1)S(1)} collective-permute-done((bf16[144,896]{1,0:T(8,128)(2,1)S(1)}, bf16[144,896]{1,0:T(8,128)(2,1)S(1)}, u32[]{:S(2)}, u32[]{:S(2)}) %collective-permute-start.37) | collective-permute-done | bytes 258080 | tf_op jit(solution)/shard_map/ppermute | solution.py:19
  187.6 11.6 %collective-permute-done.42.refs_0_ = bf16[144,896]{1,0:T(8,128)(2,1)S(1)} collective-permute-done((bf16[144,896]{1,0:T(8,128)(2,1)S(1)}, bf16[144,896]{1,0:T(8,128)(2,1)S(1)}, u32[]{:S(2)}, u32[]{:S(2)}) %collective-permute-start.42) | collective-permute-done | bytes 258080 | tf_op jit(solution)/shard_map/ppermute | solution.py:19
  199.1 5.0 %collective-permute-start.50 = (bf16[144,896]{1,0:T(8,128)(2,1)S(1)}, bf16[144,896]{1,0:T(8,128)(2,1)S(1)}, u32[]{:S(2)}, u32[]{:S(2)}) collective-permute-start(bf16[144,896]{1,0:T(8,128)(2,1)S(1)} %fusion.53), channel_id=1, source_target_pairs={{0,4},{1,5},{2,6},{3,7},{4,0},{5,1},{6,2},{7,3},{8,12},{9,13},{10,... | collective-permute-start | bytes 774152 | tf_op jit(solution)/shard_map/ppermute | solution.py:19
  205.1 6.9 %collective-permute-done.50.refs_0_ = bf16[144,896]{1,0:T(8,128)(2,1)S(1)} collective-permute-done((bf16[144,896]{1,0:T(8,128)(2,1)S(1)}, bf16[144,896]{1,0:T(8,128)(2,1)S(1)}, u32[]{:S(2)}, u32[]{:S(2)}) %collective-permute-start.50) | collective-permute-done | bytes 258080 | tf_op jit(solution)/shard_map/ppermute | solution.py:19
  212.0 3.5 collective-permute-start.46
  237.8 22.6 %collective-permute-done.54.refs_1_ = bf16[128,7168]{1,0:T(8,128)(2,1)S(1)} collective-permute-done((bf16[128,7168]{1,0:T(8,128)(2,1)S(1)}, bf16[128,7168]{1,0:T(8,128)(2,1)S(1)}, u32[]{:S(2)}, u32[]{:S(2)}) %collective-permute-start.54) | collective-permute-done | bytes 1835040 | tf_op jit(solution)/shard_map/ppermute | solution.py:25
  277.4 3.6 collective-permute-done.63.refs_1_
  284.3 4.2 collective-permute-done.65.refs_3_
  289.1 5.0 %collective-permute-start.66 = (bf16[144,896]{1,0:T(8,128)(2,1)S(1)}, bf16[144,896]{1,0:T(8,128)(2,1)S(1)}, u32[]{:S(2)}, u32[]{:S(2)}) collective-permute-start(bf16[144,896]{1,0:T(8,128)(2,1)S(1)} %get-tuple-element.111), channel_id=1, source_target_pairs={{0,5},{1,6},{2,7},{3,0},{4,1},{5,2},{6,3},{7,4},{8,13},{9,14},{10,... | collective-permute-start | bytes 774152 | tf_op jit(solution)/shard_map/ppermute | solution.py:19
  294.9 9.8 %collective-permute-done.72 = bf16[144,896]{1,0:T(8,128)(2,1)S(1)} collective-permute-done((bf16[144,896]{1,0:T(8,128)(2,1)S(1)}, bf16[144,896]{1,0:T(8,128)(2,1)S(1)}, u32[]{:S(2)}, u32[]{:S(2)}) %collective-permute-start.72) | collective-permute-done | bytes 258080 | tf_op jit(solution)/shard_map/ppermute | solution.py:19
  316.0 5.7 %collective-permute-done.62 = bf16[144,1024]{1,0:T(8,128)(2,1)S(1)} collective-permute-done((bf16[144,1024]{1,0:T(8,128)(2,1)S(1)}, bf16[144,1024]{1,0:T(8,128)(2,1)S(1)}, u32[]{:S(2)}, u32[]{:S(2)}) %collective-permute-start.62) | collective-permute-done | bytes 294944 | tf_op jit(solution)/shard_map/ppermute | solution.py:19
  321.8 3.3 collective-permute-done.74
  328.2 5.2 %collective-permute-done.76 = bf16[144,896]{1,0:T(8,128)(2,1)S(1)} collective-permute-done((bf16[144,896]{1,0:T(8,128)(2,1)S(1)}, bf16[144,896]{1,0:T(8,128)(2,1)S(1)}, u32[]{:S(2)}, u32[]{:S(2)}) %collective-permute-start.76) | collective-permute-done | bytes 258080 | tf_op jit(solution)/shard_map/ppermute | solution.py:19
  337.3 3.7 collective-permute-done.82
  346.8 3.7 collective-permute-done.75
  361.0 4.3 collective-permute-done.77.low_down
  369.8 4.4 collective-permute-start.85
  374.2 4.6 collective-permute-done.85
  378.8 4.7 collective-permute-start.89
  384.9 3.3 collective-permute-start.88
  394.7 8.2 %collective-permute-done.91 = bf16[144,1024]{1,0:T(8,128)(2,1)S(1)} collective-permute-done((bf16[144,1024]{1,0:T(8,128)(2,1)S(1)}, bf16[144,1024]{1,0:T(8,128)(2,1)S(1)}, u32[]{:S(2)}, u32[]{:S(2)}) %collective-permute-start.91) | collective-permute-done | bytes 294944 | tf_op jit(solution)/shard_map/ppermute | solution.py:19
  403.3 3.4 collective-permute-start.92
  408.0 3.5 collective-permute-done.92.refs_4_
  411.7 5.5 %collective-permute-start.93 = (bf16[5,48,896]{2,1,0:T(8,128)(2,1)S(1)}, bf16[5,48,896]{2,1,0:T(8,128)(2,1)S(1)}, u32[]{:S(2)}, u32[]{:S(2)}) collective-permute-start(bf16[5,48,896]{2,1,0:T(8,128)(2,1)S(1)} %get-tuple-element.118), channel_id=1, source_target_pairs={{0,24},{8,0},{16,8},{24,16},{1,25},{9,1},{17,9},{25,17},{2,26},{10... | collective-permute-start | bytes 1290248 | tf_op jit(solution)/shard_map/ppermute | solution.py:19
  418.2 6.8 %collective-permute-start.103 = (bf16[144,512]{1,0:T(8,128)(2,1)S(1)}, bf16[144,512]{1,0:T(8,128)(2,1)S(1)}, u32[]{:S(2)}, u32[]{:S(2)}) collective-permute-start(bf16[144,512]{1,0:T(8,128)(2,1)S(1)} %slice.162), channel_id=1, source_target_pairs={{0,1},{1,2},{2,3},{3,4},{4,5},{5,6},{6,7},{7,0},{8,9},{9,10},{10,1... | collective-permute-start | bytes 442376 | tf_op jit(solution)/shard_map/ppermute | solution.py:19
  428.5 3.9 collective-permute-start.97
  434.8 12.5 %collective-permute-done.97.refs_0_ = bf16[144,896]{1,0:T(8,128)(2,1)S(1)} collective-permute-done((bf16[144,896]{1,0:T(8,128)(2,1)S(1)}, bf16[144,896]{1,0:T(8,128)(2,1)S(1)}, u32[]{:S(2)}, u32[]{:S(2)}) %collective-permute-start.97) | collective-permute-done | bytes 258080 | tf_op jit(solution)/shard_map/ppermute | solution.py:19
  447.3 5.6 %collective-permute-start.105 = (bf16[144,896]{1,0:T(8,128)(2,1)S(1)}, bf16[144,896]{1,0:T(8,128)(2,1)S(1)}, u32[]{:S(2)}, u32[]{:S(2)}) collective-permute-start(bf16[144,896]{1,0:T(8,128)(2,1)S(1)} %fusion.77), channel_id=1, source_target_pairs={{0,4},{1,5},{2,6},{3,7},{4,0},{5,1},{6,2},{7,3},{8,12},{9,13},{10,... | collective-permute-start | bytes 774152 | tf_op jit(solution)/shard_map/ppermute | solution.py:19
  453.0 5.0 %collective-permute-start.101 = (bf16[2,48,896]{2,1,0:T(8,128)(2,1)S(1)}, bf16[2,48,896]{2,1,0:T(8,128)(2,1)S(1)}, u32[]{:S(2)}, u32[]{:S(2)}) collective-permute-start(bf16[2,48,896]{2,1,0:T(8,128)(2,1)S(1)} %get-tuple-element.123), channel_id=1, source_target_pairs={{0,16},{8,24},{16,0},{24,8},{1,17},{9,25},{17,1},{25,9},{2,18},{10... | collective-permute-start | bytes 516104 | tf_op jit(solution)/shard_map/ppermute | solution.py:19
  460.4 3.5 collective-permute-start.102
  471.7 3.4 shard_map.90
  (285 shorter events, 205.0 us)
Async XLA Ops:
  17.3 26.8 %collective-permute-start.6 = (bf16[144,896]{1,0:T(8,128)(2,1)S(1)}, bf16[144,896]{1,0:T(8,128)(2,1)}, u32[]{:S(2)}, u32[]{:S(2)}) collective-permute-start(bf16[144,896]{1,0:T(8,128)(2,1)S(1)} %shard_map.75), channel_id=1, source_target_pairs={{0,4},{1,5},{2,6},{3,7},{4,0},{5,1},{6,2},{7,3},{8,12},{9,13},{10,... | collective-permute-start | bytes 774152 | tf_op jit(solution)/shard_map/ppermute | solution.py:19
  28.8 26.1 %collective-permute-start = (bf16[5,48,896]{2,1,0:T(8,128)(2,1)}, bf16[5,48,896]{2,1,0:T(8,128)(2,1)S(1)}, u32[]{:S(2)}, u32[]{:S(2)}) collective-permute-start(bf16[5,48,896]{2,1,0:T(8,128)(2,1)} %get-tuple-element.68), channel_id=1, source_target_pairs={{0,8},{8,16},{16,24},{24,0},{1,9},{9,17},{17,25},{25,1},{2,10},{10... | collective-permute-start | bytes 1290248 | tf_op jit(solution)/shard_map/ppermute | solution.py:19
  38.4 16.6 %collective-permute-start.1 = (bf16[5,48,896]{2,1,0:T(8,128)(2,1)}, bf16[5,48,896]{2,1,0:T(8,128)(2,1)S(1)}, u32[]{:S(2)}, u32[]{:S(2)}) collective-permute-start(bf16[5,48,896]{2,1,0:T(8,128)(2,1)} %copy-done.13), channel_id=1, source_target_pairs={{0,16},{8,24},{16,0},{24,8},{1,17},{9,25},{17,1},{25,9},{2,18},{10... | collective-permute-start | bytes 1290248 | tf_op jit(solution)/shard_map/ppermute | solution.py:19
  39.0 18.2 %collective-permute-start.2 = (bf16[5,48,896]{2,1,0:T(8,128)(2,1)}, bf16[5,48,896]{2,1,0:T(8,128)(2,1)S(1)}, u32[]{:S(2)}, u32[]{:S(2)}) collective-permute-start(bf16[5,48,896]{2,1,0:T(8,128)(2,1)} %copy-done.12), channel_id=1, source_target_pairs={{0,24},{8,0},{16,8},{24,16},{1,25},{9,1},{17,9},{25,17},{2,26},{10... | collective-permute-start | bytes 1290248 | tf_op jit(solution)/shard_map/ppermute | solution.py:19
  42.1 18.3 %collective-permute-start.17 = (bf16[144,896]{1,0:T(8,128)(2,1)S(1)}, bf16[144,896]{1,0:T(8,128)(2,1)S(1)}, u32[]{:S(2)}, u32[]{:S(2)}) collective-permute-start(bf16[144,896]{1,0:T(8,128)(2,1)S(1)} %get-tuple-element.83), channel_id=1, source_target_pairs={{0,3},{1,4},{2,5},{3,6},{4,7},{5,0},{6,1},{7,2},{8,11},{9,12},{10,... | collective-permute-start | bytes 774152 | tf_op jit(solution)/shard_map/ppermute | solution.py:19
  44.1 17.9 %collective-permute-start.11 = (bf16[144,896]{1,0:T(8,128)(2,1)S(1)}, bf16[144,896]{1,0:T(8,128)(2,1)S(1)}, u32[]{:S(2)}, u32[]{:S(2)}) collective-permute-start(bf16[144,896]{1,0:T(8,128)(2,1)S(1)} %get-tuple-element.80), channel_id=1, source_target_pairs={{0,5},{1,6},{2,7},{3,0},{4,1},{5,2},{6,3},{7,4},{8,13},{9,14},{10,... | collective-permute-start | bytes 774152 | tf_op jit(solution)/shard_map/ppermute | solution.py:19
  54.9 15.5 %collective-permute-start.26 = (bf16[144,1024]{1,0:T(8,128)(2,1)S(1)}, bf16[144,1024]{1,0:T(8,128)(2,1)S(1)}, u32[]{:S(2)}, u32[]{:S(2)}) collective-permute-start(bf16[144,1024]{1,0:T(8,128)(2,1)S(1)} %get-tuple-element.147), channel_id=1, source_target_pairs={{0,7},{1,0},{2,1},{3,2},{4,3},{5,4},{6,5},{7,6},{8,15},{9,8},{10,9... | collective-permute-start | bytes 884744 | tf_op jit(solution)/shard_map/ppermute | solution.py:19
  55.0 16.3 %collective-permute-start.7 = (bf16[144,1024]{1,0:T(8,128)(2,1)S(1)}, bf16[144,1024]{1,0:T(8,128)(2,1)S(1)}, u32[]{:S(2)}, u32[]{:S(2)}) collective-permute-start(bf16[144,1024]{1,0:T(8,128)(2,1)S(1)} %get-tuple-element.148), channel_id=1, source_target_pairs={{0,1},{1,2},{2,3},{3,4},{4,5},{5,6},{6,7},{7,0},{8,9},{9,10},{10,1... | collective-permute-start | bytes 884744 | tf_op jit(solution)/shard_map/ppermute | solution.py:19
  57.4 21.5 %collective-permute-start.19 = (bf16[144,896]{1,0:T(8,128)(2,1)S(1)}, bf16[144,896]{1,0:T(8,128)(2,1)S(1)}, u32[]{:S(2)}, u32[]{:S(2)}) collective-permute-start(bf16[144,896]{1,0:T(8,128)(2,1)S(1)} %get-tuple-element.84), channel_id=1, source_target_pairs={{0,2},{1,3},{2,4},{3,5},{4,6},{5,7},{6,0},{7,1},{8,10},{9,11},{10,... | collective-permute-start | bytes 774152 | tf_op jit(solution)/shard_map/ppermute | solution.py:19
  61.3 26.8 %collective-permute-start.18 = (bf16[144,1024]{1,0:T(8,128)(2,1)S(1)}, bf16[144,1024]{1,0:T(8,128)(2,1)S(1)}, u32[]{:S(2)}, u32[]{:S(2)}) collective-permute-start(bf16[144,1024]{1,0:T(8,128)(2,1)S(1)} %slice.231), channel_id=1, source_target_pairs={{0,7},{1,0},{2,1},{3,2},{4,3},{5,4},{6,5},{7,6},{8,15},{9,8},{10,9... | collective-permute-start | bytes 884744 | tf_op jit(solution)/shard_map/ppermute | solution.py:19
  62.1 21.8 %collective-permute-start.21 = (bf16[144,896]{1,0:T(8,128)(2,1)S(1)}, bf16[144,896]{1,0:T(8,128)(2,1)S(1)}, u32[]{:S(2)}, u32[]{:S(2)}) collective-permute-start(bf16[144,896]{1,0:T(8,128)(2,1)S(1)} %get-tuple-element.85), channel_id=1, source_target_pairs={{0,1},{1,2},{2,3},{3,4},{4,5},{5,6},{6,7},{7,0},{8,9},{9,10},{10,1... | collective-permute-start | bytes 774152 | tf_op jit(solution)/shard_map/ppermute | solution.py:19
  70.3 16.0 %collective-permute-start.13 = (bf16[144,896]{1,0:T(8,128)(2,1)S(1)}, bf16[144,896]{1,0:T(8,128)(2,1)S(1)}, u32[]{:S(2)}, u32[]{:S(2)}) collective-permute-start(bf16[144,896]{1,0:T(8,128)(2,1)S(1)} %get-tuple-element.81), channel_id=1, source_target_pairs={{0,6},{1,7},{2,0},{3,1},{4,2},{5,3},{6,4},{7,5},{8,14},{9,15},{10,... | collective-permute-start | bytes 774152 | tf_op jit(solution)/shard_map/ppermute | solution.py:19
  71.3 28.8 %collective-permute-start.23 = (bf16[144,1024]{1,0:T(8,128)(2,1)S(1)}, bf16[144,1024]{1,0:T(8,128)(2,1)S(1)}, u32[]{:S(2)}, u32[]{:S(2)}) collective-permute-start(bf16[144,1024]{1,0:T(8,128)(2,1)S(1)} %slice.230), channel_id=1, source_target_pairs={{0,1},{1,2},{2,3},{3,4},{4,5},{5,6},{6,7},{7,0},{8,9},{9,10},{10,1... | collective-permute-start | bytes 884744 | tf_op jit(solution)/shard_map/ppermute | solution.py:19
  78.9 23.7 %collective-permute-start.15 = (bf16[144,896]{1,0:T(8,128)(2,1)S(1)}, bf16[144,896]{1,0:T(8,128)(2,1)S(1)}, u32[]{:S(2)}, u32[]{:S(2)}) collective-permute-start(bf16[144,896]{1,0:T(8,128)(2,1)S(1)} %get-tuple-element.82), channel_id=1, source_target_pairs={{0,7},{1,0},{2,1},{3,2},{4,3},{5,4},{6,5},{7,6},{8,15},{9,8},{10,9... | collective-permute-start | bytes 774152 | tf_op jit(solution)/shard_map/ppermute | solution.py:19
  100.3 15.9 %collective-permute-start.14 = (bf16[144,1024]{1,0:T(8,128)(2,1)S(1)}, bf16[144,1024]{1,0:T(8,128)(2,1)S(1)}, u32[]{:S(2)}, u32[]{:S(2)}) collective-permute-start(bf16[144,1024]{1,0:T(8,128)(2,1)S(1)} %get-tuple-element.144), channel_id=1, source_target_pairs={{0,1},{1,2},{2,3},{3,4},{4,5},{5,6},{6,7},{7,0},{8,9},{9,10},{10,1... | collective-permute-start | bytes 884744 | tf_op jit(solution)/shard_map/ppermute | solution.py:19
  140.0 21.1 %collective-permute-start.31 = (bf16[144,896]{1,0:T(8,128)(2,1)S(1)}, bf16[144,896]{1,0:T(8,128)(2,1)S(1)}, u32[]{:S(2)}, u32[]{:S(2)}) collective-permute-start(bf16[144,896]{1,0:T(8,128)(2,1)S(1)} %fusion.35), channel_id=1, source_target_pairs={{0,1},{1,2},{2,3},{3,4},{4,5},{5,6},{6,7},{7,0},{8,9},{9,10},{10,1... | collective-permute-start | bytes 774152 | tf_op jit(solution)/shard_map/ppermute | solution.py:19
  142.1 18.5 %collective-permute-start.36 = (bf16[144,1024]{1,0:T(8,128)(2,1)S(1)}, bf16[144,1024]{1,0:T(8,128)(2,1)S(1)}, u32[]{:S(2)}, u32[]{:S(2)}) collective-permute-start(bf16[144,1024]{1,0:T(8,128)(2,1)S(1)} %collective-permute-done.32), channel_id=1, source_target_pairs={{0,1},{1,2},{2,3},{3,4},{4,5},{5,6},{6,7},{7,0},{8,9},{9,10},{10,1... | collective-permute-start | bytes 884744 | tf_op jit(solution)/shard_map/ppermute | solution.py:19
  143.3 18.8 %collective-permute-start.33 = (bf16[144,896]{1,0:T(8,128)(2,1)S(1)}, bf16[144,896]{1,0:T(8,128)(2,1)S(1)}, u32[]{:S(2)}, u32[]{:S(2)}) collective-permute-start(bf16[144,896]{1,0:T(8,128)(2,1)S(1)} %fusion.38), channel_id=1, source_target_pairs={{0,7},{1,0},{2,1},{3,2},{4,3},{5,4},{6,5},{7,6},{8,15},{9,8},{10,9... | collective-permute-start | bytes 774152 | tf_op jit(solution)/shard_map/ppermute | solution.py:19
  150.4 24.9 %collective-permute-start.41 = (bf16[144,1024]{1,0:T(8,128)(2,1)S(1)}, bf16[144,1024]{1,0:T(8,128)(2,1)S(1)}, u32[]{:S(2)}, u32[]{:S(2)}) collective-permute-start(bf16[144,1024]{1,0:T(8,128)(2,1)S(1)} %collective-permute-done.34), channel_id=1, source_target_pairs={{0,7},{1,0},{2,1},{3,2},{4,3},{5,4},{6,5},{7,6},{8,15},{9,8},{10,9... | collective-permute-start | bytes 884744 | tf_op jit(solution)/shard_map/ppermute | solution.py:19
  171.4 45.4 %collective-permute-start.38 = (bf16[5,48,896]{2,1,0:T(8,128)(2,1)S(1)}, bf16[5,48,896]{2,1,0:T(8,128)(2,1)S(1)}, u32[]{:S(2)}, u32[]{:S(2)}) collective-permute-start(bf16[5,48,896]{2,1,0:T(8,128)(2,1)S(1)} %get-tuple-element.87), channel_id=1, source_target_pairs={{0,24},{8,0},{16,8},{24,16},{1,25},{9,1},{17,9},{25,17},{2,26},{10... | collective-permute-start | bytes 1290248 | tf_op jit(solution)/shard_map/ppermute | solution.py:19
  172.8 46.9 %collective-permute-start.39 = (bf16[5,48,896]{2,1,0:T(8,128)(2,1)S(1)}, bf16[5,48,896]{2,1,0:T(8,128)(2,1)S(1)}, u32[]{:S(2)}, u32[]{:S(2)}) collective-permute-start(bf16[5,48,896]{2,1,0:T(8,128)(2,1)S(1)} %get-tuple-element.88), channel_id=1, source_target_pairs={{0,16},{8,24},{16,0},{24,8},{1,17},{9,25},{17,1},{25,9},{2,18},{10... | collective-permute-start | bytes 1290248 | tf_op jit(solution)/shard_map/ppermute | solution.py:19
  174.3 46.0 %collective-permute-start.40 = (bf16[5,48,896]{2,1,0:T(8,128)(2,1)S(1)}, bf16[5,48,896]{2,1,0:T(8,128)(2,1)S(1)}, u32[]{:S(2)}, u32[]{:S(2)}) collective-permute-start(bf16[5,48,896]{2,1,0:T(8,128)(2,1)S(1)} %get-tuple-element.89), channel_id=1, source_target_pairs={{0,8},{8,16},{16,24},{24,0},{1,9},{9,17},{17,25},{25,1},{2,10},{10... | collective-permute-start | bytes 1290248 | tf_op jit(solution)/shard_map/ppermute | solution.py:19
  182.0 17.1 %collective-permute-start.42 = (bf16[144,896]{1,0:T(8,128)(2,1)S(1)}, bf16[144,896]{1,0:T(8,128)(2,1)S(1)}, u32[]{:S(2)}, u32[]{:S(2)}) collective-permute-start(bf16[144,896]{1,0:T(8,128)(2,1)S(1)} %fusion.47), channel_id=1, source_target_pairs={{0,3},{1,4},{2,5},{3,6},{4,7},{5,0},{6,1},{7,2},{8,11},{9,12},{10,... | collective-permute-start | bytes 774152 | tf_op jit(solution)/shard_map/ppermute | solution.py:19
  185.4 18.8 %collective-permute-start.44 = (bf16[144,896]{1,0:T(8,128)(2,1)S(1)}, bf16[144,896]{1,0:T(8,128)(2,1)S(1)}, u32[]{:S(2)}, u32[]{:S(2)}) collective-permute-start(bf16[144,896]{1,0:T(8,128)(2,1)S(1)} %fusion.50), channel_id=1, source_target_pairs={{0,5},{1,6},{2,7},{3,0},{4,1},{5,2},{6,3},{7,4},{8,13},{9,14},{10,... | collective-permute-start | bytes 774152 | tf_op jit(solution)/shard_map/ppermute | solution.py:19
  205.0 17.6 %collective-permute-start.45 = (bf16[2,48,896]{2,1,0:T(8,128)(2,1)S(1)}, bf16[2,48,896]{2,1,0:T(8,128)(2,1)S(1)}, u32[]{:S(2)}, u32[]{:S(2)}) collective-permute-start(bf16[2,48,896]{2,1,0:T(8,128)(2,1)S(1)} %get-tuple-element.91), channel_id=1, source_target_pairs={{0,24},{8,0},{16,8},{24,16},{1,25},{9,1},{17,9},{25,17},{2,26},{10... | collective-permute-start | bytes 516104 | tf_op jit(solution)/shard_map/ppermute | solution.py:19
  235.7 24.8 %collective-permute-start.54 = (bf16[128,7168]{1,0:T(8,128)(2,1)S(1)}, bf16[128,7168]{1,0:T(8,128)(2,1)S(1)}, u32[]{:S(2)}, u32[]{:S(2)}) collective-permute-start(bf16[128,7168]{1,0:T(8,128)(2,1)S(1)} %shard_map.81.refs_4_), channel_id=1, source_target_pairs={{0,32},{32,64},{64,96},{96,128},{128,160},{160,192},{192,224},{1,3... | collective-permute-start | bytes 5505032 | tf_op jit(solution)/shard_map/ppermute | solution.py:25
  270.2 18.8 %collective-permute-start.61 = (bf16[144,896]{1,0:T(8,128)(2,1)S(1)}, bf16[144,896]{1,0:T(8,128)(2,1)S(1)}, u32[]{:S(2)}, u32[]{:S(2)}) collective-permute-start(bf16[144,896]{1,0:T(8,128)(2,1)S(1)} %shard_map.84), channel_id=1, source_target_pairs={{0,4},{1,5},{2,6},{3,7},{4,0},{5,1},{6,2},{7,3},{8,12},{9,13},{10,... | collective-permute-start | bytes 774152 | tf_op jit(solution)/shard_map/ppermute | solution.py:19
  275.6 29.9 %collective-permute-start.55 = (bf16[5,48,896]{2,1,0:T(8,128)(2,1)S(1)}, bf16[5,48,896]{2,1,0:T(8,128)(2,1)S(1)}, u32[]{:S(2)}, u32[]{:S(2)}) collective-permute-start(bf16[5,48,896]{2,1,0:T(8,128)(2,1)S(1)} %get-tuple-element.99), channel_id=1, source_target_pairs={{0,8},{8,16},{16,24},{24,0},{1,9},{9,17},{17,25},{25,1},{2,10},{10... | collective-permute-start | bytes 1290248 | tf_op jit(solution)/shard_map/ppermute | solution.py:19
  281.0 26.7 %collective-permute-start.56 = (bf16[5,48,896]{2,1,0:T(8,128)(2,1)S(1)}, bf16[5,48,896]{2,1,0:T(8,128)(2,1)S(1)}, u32[]{:S(2)}, u32[]{:S(2)}) collective-permute-start(bf16[5,48,896]{2,1,0:T(8,128)(2,1)S(1)} %get-tuple-element.100), channel_id=1, source_target_pairs={{0,16},{8,24},{16,0},{24,8},{1,17},{9,25},{17,1},{25,9},{2,18},{10... | collective-permute-start | bytes 1290248 | tf_op jit(solution)/shard_map/ppermute | solution.py:19
  284.3 24.6 %collective-permute-start.57 = (bf16[5,48,896]{2,1,0:T(8,128)(2,1)S(1)}, bf16[5,48,896]{2,1,0:T(8,128)(2,1)S(1)}, u32[]{:S(2)}, u32[]{:S(2)}) collective-permute-start(bf16[5,48,896]{2,1,0:T(8,128)(2,1)S(1)} %get-tuple-element.101), channel_id=1, source_target_pairs={{0,24},{8,0},{16,8},{24,16},{1,25},{9,1},{17,9},{25,17},{2,26},{10... | collective-permute-start | bytes 1290248 | tf_op jit(solution)/shard_map/ppermute | solution.py:19
  288.6 16.2 %collective-permute-start.72 = (bf16[144,896]{1,0:T(8,128)(2,1)S(1)}, bf16[144,896]{1,0:T(8,128)(2,1)S(1)}, u32[]{:S(2)}, u32[]{:S(2)}) collective-permute-start(bf16[144,896]{1,0:T(8,128)(2,1)S(1)} %get-tuple-element.114), channel_id=1, source_target_pairs={{0,3},{1,4},{2,5},{3,6},{4,7},{5,0},{6,1},{7,2},{8,11},{9,12},{10,... | collective-permute-start | bytes 774152 | tf_op jit(solution)/shard_map/ppermute | solution.py:19
  289.1 20.4 %collective-permute-start.66 = (bf16[144,896]{1,0:T(8,128)(2,1)S(1)}, bf16[144,896]{1,0:T(8,128)(2,1)S(1)}, u32[]{:S(2)}, u32[]{:S(2)}) collective-permute-start(bf16[144,896]{1,0:T(8,128)(2,1)S(1)} %get-tuple-element.111), channel_id=1, source_target_pairs={{0,5},{1,6},{2,7},{3,0},{4,1},{5,2},{6,3},{7,4},{8,13},{9,14},{10,... | collective-permute-start | bytes 774152 | tf_op jit(solution)/shard_map/ppermute | solution.py:19
  305.6 16.1 %collective-permute-start.62 = (bf16[144,1024]{1,0:T(8,128)(2,1)S(1)}, bf16[144,1024]{1,0:T(8,128)(2,1)S(1)}, u32[]{:S(2)}, u32[]{:S(2)}) collective-permute-start(bf16[144,1024]{1,0:T(8,128)(2,1)S(1)} %get-tuple-element.146), channel_id=1, source_target_pairs={{0,1},{1,2},{2,3},{3,4},{4,5},{5,6},{6,7},{7,0},{8,9},{9,10},{10,1... | collective-permute-start | bytes 884744 | tf_op jit(solution)/shard_map/ppermute | solution.py:19
  307.7 29.7 %collective-permute-start.73 = (bf16[144,1024]{1,0:T(8,128)(2,1)S(1)}, bf16[144,1024]{1,0:T(8,128)(2,1)S(1)}, u32[]{:S(2)}, u32[]{:S(2)}) collective-permute-start(bf16[144,1024]{1,0:T(8,128)(2,1)S(1)} %slice.229), channel_id=1, source_target_pairs={{0,7},{1,0},{2,1},{3,2},{4,3},{5,4},{6,5},{7,6},{8,15},{9,8},{10,9... | collective-permute-start | bytes 884744 | tf_op jit(solution)/shard_map/ppermute | solution.py:19
  309.0 16.0 %collective-permute-start.74 = (bf16[144,896]{1,0:T(8,128)(2,1)S(1)}, bf16[144,896]{1,0:T(8,128)(2,1)S(1)}, u32[]{:S(2)}, u32[]{:S(2)}) collective-permute-start(bf16[144,896]{1,0:T(8,128)(2,1)S(1)} %get-tuple-element.115), channel_id=1, source_target_pairs={{0,2},{1,3},{2,4},{3,5},{4,6},{5,7},{6,0},{7,1},{8,10},{9,11},{10,... | collective-permute-start | bytes 774152 | tf_op jit(solution)/shard_map/ppermute | solution.py:19
  309.4 23.9 %collective-permute-start.76 = (bf16[144,896]{1,0:T(8,128)(2,1)S(1)}, bf16[144,896]{1,0:T(8,128)(2,1)S(1)}, u32[]{:S(2)}, u32[]{:S(2)}) collective-permute-start(bf16[144,896]{1,0:T(8,128)(2,1)S(1)} %get-tuple-element.116), channel_id=1, source_target_pairs={{0,1},{1,2},{2,3},{3,4},{4,5},{5,6},{6,7},{7,0},{8,9},{9,10},{10,1... | collective-permute-start | bytes 774152 | tf_op jit(solution)/shard_map/ppermute | solution.py:19
  314.7 29.2 %collective-permute-start.78 = (bf16[144,1024]{1,0:T(8,128)(2,1)S(1)}, bf16[144,1024]{1,0:T(8,128)(2,1)S(1)}, u32[]{:S(2)}, u32[]{:S(2)}) collective-permute-start(bf16[144,1024]{1,0:T(8,128)(2,1)S(1)} %slice.228), channel_id=1, source_target_pairs={{0,1},{1,2},{2,3},{3,4},{4,5},{5,6},{6,7},{7,0},{8,9},{9,10},{10,1... | collective-permute-start | bytes 884744 | tf_op jit(solution)/shard_map/ppermute | solution.py:19
  325.0 21.0 %collective-permute-start.70 = (bf16[144,896]{1,0:T(8,128)(2,1)S(1)}, bf16[144,896]{1,0:T(8,128)(2,1)S(1)}, u32[]{:S(2)}, u32[]{:S(2)}) collective-permute-start(bf16[144,896]{1,0:T(8,128)(2,1)S(1)} %get-tuple-element.113), channel_id=1, source_target_pairs={{0,7},{1,0},{2,1},{3,2},{4,3},{5,4},{6,5},{7,6},{8,15},{9,8},{10,9... | collective-permute-start | bytes 774152 | tf_op jit(solution)/shard_map/ppermute | solution.py:19
  384.0 19.3 %collective-permute-start.86 = (bf16[144,896]{1,0:T(8,128)(2,1)S(1)}, bf16[144,896]{1,0:T(8,128)(2,1)S(1)}, u32[]{:S(2)}, u32[]{:S(2)}) collective-permute-start(bf16[144,896]{1,0:T(8,128)(2,1)S(1)} %fusion.59), channel_id=1, source_target_pairs={{0,1},{1,2},{2,3},{3,4},{4,5},{5,6},{6,7},{7,0},{8,9},{9,10},{10,1... | collective-permute-start | bytes 774152 | tf_op jit(solution)/shard_map/ppermute | solution.py:19
  384.3 18.5 %collective-permute-start.91 = (bf16[144,1024]{1,0:T(8,128)(2,1)S(1)}, bf16[144,1024]{1,0:T(8,128)(2,1)S(1)}, u32[]{:S(2)}, u32[]{:S(2)}) collective-permute-start(bf16[144,1024]{1,0:T(8,128)(2,1)S(1)} %collective-permute-done.87), channel_id=1, source_target_pairs={{0,1},{1,2},{2,3},{3,4},{4,5},{5,6},{6,7},{7,0},{8,9},{9,10},{10,1... | collective-permute-start | bytes 884744 | tf_op jit(solution)/shard_map/ppermute | solution.py:19
  384.9 22.3 %collective-permute-start.88 = (bf16[144,896]{1,0:T(8,128)(2,1)S(1)}, bf16[144,896]{1,0:T(8,128)(2,1)S(1)}, u32[]{:S(2)}, u32[]{:S(2)}) collective-permute-start(bf16[144,896]{1,0:T(8,128)(2,1)S(1)} %fusion.62), channel_id=1, source_target_pairs={{0,7},{1,0},{2,1},{3,2},{4,3},{5,4},{6,5},{7,6},{8,15},{9,8},{10,9... | collective-permute-start | bytes 774152 | tf_op jit(solution)/shard_map/ppermute | solution.py:19
  390.8 17.2 %collective-permute-start.90 = (bf16[144,896]{1,0:T(8,128)(2,1)S(1)}, bf16[144,896]{1,0:T(8,128)(2,1)S(1)}, u32[]{:S(2)}, u32[]{:S(2)}) collective-permute-start(bf16[144,896]{1,0:T(8,128)(2,1)S(1)} %fusion.65), channel_id=1, source_target_pairs={{0,2},{1,3},{2,4},{3,5},{4,6},{5,7},{6,0},{7,1},{8,10},{9,11},{10,... | collective-permute-start | bytes 774152 | tf_op jit(solution)/shard_map/ppermute | solution.py:19
  393.4 31.6 %collective-permute-start.96 = (bf16[144,1024]{1,0:T(8,128)(2,1)S(1)}, bf16[144,1024]{1,0:T(8,128)(2,1)S(1)}, u32[]{:S(2)}, u32[]{:S(2)}) collective-permute-start(bf16[144,1024]{1,0:T(8,128)(2,1)S(1)} %collective-permute-done.89), channel_id=1, source_target_pairs={{0,7},{1,0},{2,1},{3,2},{4,3},{5,4},{6,5},{7,6},{8,15},{9,8},{10,9... | collective-permute-start | bytes 884744 | tf_op jit(solution)/shard_map/ppermute | solution.py:19
  411.7 41.3 %collective-permute-start.93 = (bf16[5,48,896]{2,1,0:T(8,128)(2,1)S(1)}, bf16[5,48,896]{2,1,0:T(8,128)(2,1)S(1)}, u32[]{:S(2)}, u32[]{:S(2)}) collective-permute-start(bf16[5,48,896]{2,1,0:T(8,128)(2,1)S(1)} %get-tuple-element.118), channel_id=1, source_target_pairs={{0,24},{8,0},{16,8},{24,16},{1,25},{9,1},{17,9},{25,17},{2,26},{10... | collective-permute-start | bytes 1290248 | tf_op jit(solution)/shard_map/ppermute | solution.py:19
  417.2 46.6 %collective-permute-start.94 = (bf16[5,48,896]{2,1,0:T(8,128)(2,1)S(1)}, bf16[5,48,896]{2,1,0:T(8,128)(2,1)S(1)}, u32[]{:S(2)}, u32[]{:S(2)}) collective-permute-start(bf16[5,48,896]{2,1,0:T(8,128)(2,1)S(1)} %get-tuple-element.119), channel_id=1, source_target_pairs={{0,16},{8,24},{16,0},{24,8},{1,17},{9,25},{17,1},{25,9},{2,18},{10... | collective-permute-start | bytes 1290248 | tf_op jit(solution)/shard_map/ppermute | solution.py:19
  417.8 46.1 %collective-permute-start.95 = (bf16[5,48,896]{2,1,0:T(8,128)(2,1)S(1)}, bf16[5,48,896]{2,1,0:T(8,128)(2,1)S(1)}, u32[]{:S(2)}, u32[]{:S(2)}) collective-permute-start(bf16[5,48,896]{2,1,0:T(8,128)(2,1)S(1)} %get-tuple-element.120), channel_id=1, source_target_pairs={{0,8},{8,16},{16,24},{24,0},{1,9},{9,17},{17,25},{25,1},{2,10},{10... | collective-permute-start | bytes 1290248 | tf_op jit(solution)/shard_map/ppermute | solution.py:19
  428.5 18.8 %collective-permute-start.97 = (bf16[144,896]{1,0:T(8,128)(2,1)S(1)}, bf16[144,896]{1,0:T(8,128)(2,1)S(1)}, u32[]{:S(2)}, u32[]{:S(2)}) collective-permute-start(bf16[144,896]{1,0:T(8,128)(2,1)S(1)} %fusion.71), channel_id=1, source_target_pairs={{0,3},{1,4},{2,5},{3,6},{4,7},{5,0},{6,1},{7,2},{8,11},{9,12},{10,... | collective-permute-start | bytes 774152 | tf_op jit(solution)/shard_map/ppermute | solution.py:19
  432.4 20.4 %collective-permute-start.99 = (bf16[144,896]{1,0:T(8,128)(2,1)S(1)}, bf16[144,896]{1,0:T(8,128)(2,1)S(1)}, u32[]{:S(2)}, u32[]{:S(2)}) collective-permute-start(bf16[144,896]{1,0:T(8,128)(2,1)S(1)} %fusion.74), channel_id=1, source_target_pairs={{0,5},{1,6},{2,7},{3,0},{4,1},{5,2},{6,3},{7,4},{8,13},{9,14},{10,... | collective-permute-start | bytes 774152 | tf_op jit(solution)/shard_map/ppermute | solution.py:19
  (78 other events, 953.3 us)
